TPU v7x, 32 devices: a whole 2x2x4 slice. The times are simulated.
32 devices in a mesh: dp: 4 (over y, x), ctx: 8 (over z, core).
Axes of the slice: x: 2, y: 2, z: 4, core: 2. Of those that a mesh axis runs over, the one named last changes fastest.
Arguments:
- tokens: bfloat16 [8192, 2048], P(('dp', 'ctx')), may hold values from -6 to 6
- in_weight: bfloat16 [3, 2048, 2048], P(None, ('dp', 'ctx')), may hold values from -0.125 to 0.125
- short_taps: float32 [7, 3, 2048], replicated, may hold values from -2.4 to 2.4
- long_taps: bfloat16 [128, 128], replicated, may hold values from -0.5 to 0.5
- out_weight: bfloat16 [2048, 2048], P(('dp', 'ctx')), may hold values from -0.125 to 0.125
Outputs:
- block_out: bfloat16 [8192, 2048], P(('dp', 'ctx'))
All inputs are finite; a program needn't handle non-finite values.
Results may differ from a plain program's by a relative error of at most 0.0076.
Values may be sent and summed in bfloat16 or wider, within the bound.
No kernel may reach another device: no remote copies, remote signals or barrier semaphores. Data moves between devices by JAX's collectives and lax.ppermute only.
A program may use at most 128 MiB of HBM per device.

v0:
```python
import functools

import jax
import jax.numpy as jnp
from jax import lax
from jax.experimental import pallas as pl
from jax.experimental.pallas import tpu as pltpu
from jax.sharding import Mesh
from jax.sharding import PartitionSpec as P

GSIZE = 16
SHORT = 7
TAPS = 128
EDGE = 144
LANES = 128
LEAD = 256
ANY = pl.BlockSpec(memory_space=pl.ANY)
SMEM = pl.BlockSpec(memory_space=pltpu.SMEM)
VMEM = pl.BlockSpec(memory_space=pltpu.VMEM)


def ring_of(count):
    order = [i for i in range(count) if i == 0 or i % 2 == 1]
    order += [i for i in reversed(range(1, count)) if i % 2 == 0]
    return [(order[i], order[(i + 1) % count]) for i in range(count)]


def origins_of(count):
    previous = dict((target, source) for source, target in ring_of(count))
    table = [list(range(count))]
    for _ in range(count - 1):
        table.append([previous[i] for i in table[-1]])
    return table


def swap(block):
    return lax.ppermute(block, "core", [(0, 1), (1, 0)])


def across(block, r):
    count = lax.axis_size("dp")
    return lax.ppermute(block, "dp", [(i, i ^ r) for i in range(count)])


def nt(a, b):
    return lax.dot_general(a, b, (((1,), (1,)), ((), ())), preferred_element_type=jnp.float32)


def tn(a, b):
    return lax.dot_general(a, b, (((0,), (0,)), ((), ())), preferred_element_type=jnp.float32)


def rounded(x):
    return x.astype(jnp.bfloat16).astype(jnp.float32)


def mix_kernel(places, slots, core_ref, w_ref, taps_ref, long_ref, *rest):
    pieces, rest = rest[: len(places)], rest[len(places) :]
    edges, rest = rest[:2], rest[2:]
    outs, rest = rest[:slots], rest[slots:]
    tokens, edge_tokens, streams, edge, tiles, gated, mixed, sems, edge_sems = rest
    lines = w_ref.shape[0]
    width = lines // 3
    rows = tokens.shape[2]
    half = edge_tokens.shape[3]
    size = min(width, GSIZE)
    count = width // size
    core = core_ref[0]

    copies = []
    for n, (slot, side, row) in enumerate(places):
        part = pieces[n]
        copies.append(
            (
                slot,
                pltpu.make_async_copy(
                    part, tokens.at[slot, side, pl.ds(row, part.shape[0])], sems.at[n]
                ),
            )
        )
    edge_copies = [
        pltpu.make_async_copy(edges[side], edge_tokens.at[side], edge_sems.at[side])
        for side in range(2)
    ]
    for copy in edge_copies:
        copy.start()
    for slot in range(slots):
        for owner, copy in copies:
            if owner == slot:
                copy.start()

    for g in range(count):
        line = jnp.concatenate(
            [jnp.zeros((1, TAPS), jnp.float32), long_ref[g : g + 1, :]], axis=1
        )
        square = pltpu.roll(
            jnp.broadcast_to(line, (2 * TAPS, 2 * TAPS)), 0, 1, stride=1, stride_axis=0
        )
        tiles[g] = square[:, :TAPS].astype(jnp.bfloat16)
    edge[...] = jnp.zeros_like(edge)
    for copy in edge_copies:
        copy.wait()

    total = LEAD + 2 * rows
    step = min(8, width)
    blocks = 2 * rows // TAPS
    mine = pl.multiple_of(LEAD + core * rows, LANES)
    theirs = pl.multiple_of(LEAD + (1 - core) * rows, LANES)
    w_mine = pl.ds(pl.multiple_of(core * half, LANES), half)
    w_theirs = pl.ds(pl.multiple_of((1 - core) * half, LANES), half)

    def feat(k, r, first):
        base = k * width + r
        x = streams[base : base + step, first - LANES : total]
        taps = taps_ref[base : base + step, :]
        acc = None
        for j in range(SHORT):
            term = taps[:, j : j + 1] * (x if j == 0 else pltpu.roll(x, j, 1))
            acc = term if acc is None else acc + term
        return acc[:, LANES:]

    def one(slot, carry):
        for k in range(slots):

            @pl.when(slot == k)
            def _():
                for owner, copy in copies:
                    if owner == k:
                        copy.wait()

        w = w_ref[...]
        streams[:, pl.ds(mine, rows)] = rounded(nt(w, tokens[slot, 0]))
        streams[:, pl.ds(theirs, rows)] = rounded(nt(w, tokens[slot, 1]))
        edge[:, :EDGE] = rounded(
            nt(w_ref[:, w_mine], edge_tokens[0, slot])
            + nt(w_ref[:, w_theirs], edge_tokens[1, slot])
        )
        streams[:, :LEAD] = pltpu.roll(edge[...], LEAD - EDGE, 1)
        for r in range(0, width, step):
            gated[r : r + step, :] = feat(1, r, LANES) * feat(2, r, LANES)
        for g in range(count):
            at = g * size
            part = gated[at : at + size, :].astype(jnp.bfloat16)
            window = jnp.concatenate(
                [part[:, b * TAPS : b * TAPS + 2 * TAPS] for b in range(blocks)], axis=0
            )
            conv = jnp.dot(window, tiles[g], preferred_element_type=jnp.float32)
            wide = jnp.concatenate([conv[b * size : (b + 1) * size] for b in range(blocks)], axis=1)
            query = jnp.concatenate([feat(0, at + r, LEAD) for r in range(0, size, step)], axis=0)
            mixed[at : at + size, :] = (query * wide).astype(jnp.bfloat16)
        for k in range(slots):

            @pl.when(slot == k)
            def _():
                outs[k][...] = mixed[...]

        return carry

    lax.fori_loop(0, slots, one, 0)


def mix_chunk(core, w, taps, filters, places, pieces, edges):
    lines, features = w.shape
    width = lines // 3
    slots, _, half = edges[0].shape
    rows = max(row + p.shape[0] for (_, _, row), p in zip(places, pieces))
    count = filters.shape[0]
    return pl.pallas_call(
        functools.partial(mix_kernel, places, slots),
        out_shape=[jax.ShapeDtypeStruct((width, 2 * rows), jnp.bfloat16)] * slots,
        in_specs=[SMEM, VMEM, VMEM, VMEM] + [ANY] * (len(pieces) + 2),
        out_specs=[VMEM] * slots,
        scratch_shapes=[
            pltpu.VMEM((slots, 2, rows, features), jnp.bfloat16),
            pltpu.VMEM((2, slots, EDGE, half), jnp.bfloat16),
            pltpu.VMEM((lines, LEAD + 2 * rows), jnp.float32),
            pltpu.VMEM((lines, LEAD), jnp.float32),
            pltpu.VMEM((count, 2 * TAPS, TAPS), jnp.bfloat16),
            pltpu.VMEM((width, LANES + 2 * rows), jnp.float32),
            pltpu.VMEM((width, 2 * rows), jnp.bfloat16),
            pltpu.SemaphoreType.DMA((len(pieces),)),
            pltpu.SemaphoreType.DMA((2,)),
        ],
        compiler_params=pltpu.CompilerParams(vmem_limit_bytes=44 * 1024 * 1024),
        cost_estimate=pl.CostEstimate(
            flops=2 * slots * 2 * rows * lines * features,
            bytes_accessed=2 * slots * 2 * rows * features,
            transcendentals=0,
        ),
    )(core, w, taps, filters, *pieces, *edges)


def out_kernel(count, core_ref, *refs):
    parts, weights = refs[:count], refs[count : 2 * count]
    out_ref, left, right, sems = refs[2 * count :]
    depth = parts[0].shape[0]
    rows = out_ref.shape[0]
    copies = []
    for n in range(count):
        here = pl.ds(n * depth, depth)
        copies.append(pltpu.make_async_copy(parts[n], left.at[here], sems.at[0, n]))
        copies.append(pltpu.make_async_copy(weights[n], right.at[here], sems.at[1, n]))
    for copy in copies:
        copy.start()
    for copy in copies:
        copy.wait()
    at = pl.multiple_of(core_ref[0] * rows, LANES)
    a = left[:, pl.ds(at, rows)].T
    tile = 512
    for t in range(0, out_ref.shape[1], tile):
        out_ref[:, t : t + tile] = jnp.dot(
            a, right[:, t : t + tile], preferred_element_type=jnp.float32
        ).astype(out_ref.dtype)


def project(which, parts, weights, dtype):
    count = len(parts)
    depth, span = parts[0].shape
    width = weights[0].shape[1]
    rows = span // 2
    return pl.pallas_call(
        functools.partial(out_kernel, count),
        out_shape=jax.ShapeDtypeStruct((rows, width), dtype),
        in_specs=[SMEM] + [ANY] * (2 * count),
        out_specs=VMEM,
        scratch_shapes=[
            pltpu.VMEM((count * depth, span), jnp.bfloat16),
            pltpu.VMEM((count * depth, width), jnp.bfloat16),
            pltpu.SemaphoreType.DMA((2, count)),
        ],
        compiler_params=pltpu.CompilerParams(vmem_limit_bytes=44 * 1024 * 1024),
        cost_estimate=pl.CostEstimate(
            flops=2 * rows * width * count * depth,
            bytes_accessed=2 * count * depth * (width + span),
            transcendentals=0,
        ),
    )(which, *parts, *weights)


def tie(*groups):
    return lax.optimization_barrier(groups)


def shards(chips, tokens, in_weight, short_taps, long_taps, out_weight):
    _, width, features = in_weight.shape
    rows = tokens.shape[0]
    half = features // 2
    slots = lax.axis_size("dp")
    dp = lax.axis_index("dp")
    z = lax.axis_index("z")
    core = lax.axis_index("core")
    ring = ring_of(chips)
    forward = lambda block: lax.ppermute(block, "z", ring)

    table = jnp.array(origins_of(chips), jnp.int32)
    origins = lax.dynamic_index_in_dim(table, z, 1, False)
    core_arg = core.reshape(1).astype(jnp.int32)
    taps, filters = [], []
    for s in range(chips):
        base = ((dp * chips + origins[s]) * 2 + core) * width
        part = lax.dynamic_slice_in_dim(short_taps, base, width, 2)
        taps.append(jnp.pad(part.reshape(SHORT, 3 * width).T, ((0, 0), (0, 1))))
        filters.append(
            lax.dynamic_slice_in_dim(
                long_taps, base // GSIZE, max(1, width // GSIZE), 0
            ).astype(jnp.float32)
        )

    pairs = lambda c: [(2 * i + 1, 2 * (i + 1) + c) for i in range(chips - 1)]
    last = tokens[rows - EDGE :]
    edge = lax.ppermute(last[:, :half], ("z", "core"), pairs(0)) + lax.ppermute(
        last[:, half:], ("z", "core"), pairs(1)
    )
    ws, vs = [in_weight], [out_weight]
    ws.append(forward(ws[0]))
    vs.append(forward(vs[0]))
    blocks = [tokens] + [None] * (slots - 1)
    twins = [swap(tokens)] + [None] * (slots - 1)
    quick = slots == 4
    for r in range(1, slots):
        if not (quick and r == 3):
            blocks[r] = across(tokens, r)
    near = jnp.stack([edge] + [across(edge, r) for r in range(1, slots)])
    (blocks, twins, ws, vs, near) = tie(blocks[:3] if quick else blocks, twins[:1], ws, vs, near)

    places = [(r, 0, 0) for r in range(3 if quick else slots)]
    pieces = list(blocks)
    ws.append(forward(ws[1]))
    vs.append(forward(vs[1]))
    twins = list(twins) + [swap(block) for block in blocks[1:]]
    halves = []
    if quick:
        halves = [across(blocks[2][: rows // 2], 1), across(blocks[1][rows // 2 :], 2)]
    far = swap(near)
    spread = lambda v: [v] + [across(v, r) for r in range(1, slots)]
    wide = [None] * chips
    wide[1] = spread(vs[1])
    (twins, halves, ws, vs, far, wide[1]) = tie(twins, halves, ws, vs, far, wide[1])

    if quick:
        places += [(3, 0, 0), (3, 0, rows // 2)]
        pieces += list(halves)
    places += [(r, 1, 0) for r in range(len(twins))]
    pieces += list(twins)
    if quick:
        places += [(3, 1, 0), (3, 1, rows // 2)]
        pieces += [swap(block) for block in halves]
    for s in range(3, chips):
        ws.append(forward(ws[s - 1]))
        vs.append(forward(vs[s - 1]))
    wide[0] = spread(vs[0])
    mix = lambda s: mix_chunk(
        core_arg,
        ws[s].reshape(3 * width, features),
        taps[s],
        filters[s],
        places,
        pieces,
        (near, far),
    )
    mixed = [mix(s) for s in range(3)]
    wide[2] = spread(vs[2])
    (mixed, ws, wide[0], wide[2]) = tie(mixed, ws, wide[0], wide[2])
    mixed = list(mixed) + [mix(s) for s in range(3, chips)]
    for s in range(3, chips):
        wide[s] = spread(vs[s])
    moved = [
        [m[0]] + [across(m[r], r) for r in range(1, slots)] for m in mixed
    ]
    if width % 16:
        join = lambda lists: [jnp.concatenate([one[r] for one in lists]) for r in range(slots)]
    else:
        join = lambda lists: [one[r] for one in lists for r in range(slots)]
    parts, weights = join(moved), join(wide)
    theirs = swap(project(1 - core_arg, parts, weights, jnp.bfloat16))
    mine = project(core_arg, parts, weights, jnp.float32)
    return (mine + theirs.astype(jnp.float32)).astype(jnp.bfloat16)


def solution(mesh):
    count = mesh.shape["dp"]
    chips = mesh.shape["ctx"] // 2
    fine = Mesh(mesh.devices.reshape(count, chips, 2), ("dp", "z", "core"))
    every = ("dp", "z", "core")
    in_specs = (P(every, None), P(None, every, None), P(), P(), P(every, None))
    return jax.shard_map(
        functools.partial(shards, chips),
        mesh=fine,
        in_specs=in_specs,
        out_specs=P(every, None),
        check_vma=False,
    )
```

profile of v0, /device:TPU:0, one launch (start us, length us, event | category | flops | bytes accessed | tf_op | source)
XLA Modules:
  0.0 205.8 jit_solution(237438232174974266)
XLA Ops:
  0.0 1.2 fusion.4
  2.7 3.0 %collective-permute-start.7 = (bf16[144,1024]{1,0:T(8,128)(2,1)S(1)}, bf16[144,1024]{1,0:T(8,128)(2,1)S(1)}, u32[]{:S(2)}, u32[]{:S(2)}) collective-permute-start(bf16[144,1024]{1,0:T(8,128)(2,1)S(1)} %add.70), channel_id=1, source_target_pairs={{0,8},{8,0},{16,24},{24,16},{1,9},{9,1},{17,25},{25,17},{2,10},{10... | collective-permute-start | bytes 884744 | tf_op jit(solution)/shard_map/ppermute | solution.py:42
  5.8 2.0 collective-permute-start.1
  7.7 8.2 %collective-permute-start.2 = (bf16[256,2048]{1,0:T(8,128)(2,1)S(1)}, bf16[256,2048]{1,0:T(8,128)(2,1)S(1)}, u32[]{:S(2)}, u32[]{:S(2)}) collective-permute-start(bf16[256,2048]{1,0:T(8,128)(2,1)S(1)} %copy-done), channel_id=1, source_target_pairs={{0,1},{1,0},{2,3},{3,2},{4,5},{5,4},{6,7},{7,6},{8,9},{9,8},{10,11... | collective-permute-start | bytes 3145736 | tf_op jit(solution)/shard_map/ppermute | solution.py:37
  16.5 3.7 %collective-permute-start.3 = (bf16[3,64,2048]{2,1,0:T(8,128)(2,1)}, bf16[3,64,2048]{2,1,0:T(8,128)(2,1)S(1)}, u32[]{:S(2)}, u32[]{:S(2)}) collective-permute-start(bf16[3,64,2048]{2,1,0:T(8,128)(2,1)} %param.7), channel_id=1, source_target_pairs={{0,2},{2,6},{6,4},{4,0},{1,3},{3,7},{7,5},{5,1},{8,10},{10,14},{14... | collective-permute-start | bytes 2359304 | tf_op jit(solution)/shard_map/ppermute | solution.py:253
  20.2 9.9 %collective-permute-done.8 = bf16[144,1024]{1,0:T(8,128)(2,1)S(1)} collective-permute-done((bf16[144,1024]{1,0:T(8,128)(2,1)S(1)}, bf16[144,1024]{1,0:T(8,128)(2,1)S(1)}, u32[]{:S(2)}, u32[]{:S(2)}) %collective-permute-start.8) | collective-permute-done | bytes 294944 | tf_op jit(solution)/shard_map/ppermute | solution.py:42
  30.1 3.3 %collective-permute-start.9 = (bf16[144,1024]{1,0:T(8,128)(2,1)S(1)}, bf16[144,1024]{1,0:T(8,128)(2,1)S(1)}, u32[]{:S(2)}, u32[]{:S(2)}) collective-permute-start(bf16[144,1024]{1,0:T(8,128)(2,1)S(1)} %add.70), channel_id=1, source_target_pairs={{0,24},{8,16},{16,8},{24,0},{1,25},{9,17},{17,9},{25,1},{2,26},{10... | collective-permute-start | bytes 884744 | tf_op jit(solution)/shard_map/ppermute | solution.py:42
  33.4 7.4 %collective-permute-done.9 = bf16[144,1024]{1,0:T(8,128)(2,1)S(1)} collective-permute-done((bf16[144,1024]{1,0:T(8,128)(2,1)S(1)}, bf16[144,1024]{1,0:T(8,128)(2,1)S(1)}, u32[]{:S(2)}, u32[]{:S(2)}) %collective-permute-start.9) | collective-permute-done | bytes 294944 | tf_op jit(solution)/shard_map/ppermute | solution.py:42
  40.8 14.9 %collective-permute-start.4 = (bf16[64,2048]{1,0:T(8,128)(2,1)S(1)}, bf16[64,2048]{1,0:T(8,128)(2,1)S(1)}, u32[]{:S(2)}, u32[]{:S(2)}) collective-permute-start(bf16[64,2048]{1,0:T(8,128)(2,1)S(1)} %copy-done.8), channel_id=1, source_target_pairs={{0,2},{2,6},{6,4},{4,0},{1,3},{3,7},{7,5},{5,1},{8,10},{10,14},{14... | collective-permute-start | bytes 786440 | tf_op jit(solution)/shard_map/ppermute | solution.py:253
  55.8 7.5 %collective-permute-done.4.refs_20_ = bf16[64,2048]{1,0:T(8,128)(2,1)S(1)} collective-permute-done((bf16[64,2048]{1,0:T(8,128)(2,1)S(1)}, bf16[64,2048]{1,0:T(8,128)(2,1)S(1)}, u32[]{:S(2)}, u32[]{:S(2)}) %collective-permute-start.4) | collective-permute-done | bytes 262176 | tf_op jit(solution)/shard_map/ppermute | solution.py:253
  64.3 1.5 collective-permute-start.17
  65.8 1.5 collective-permute-start.18
  67.9 4.3 %collective-permute-done.15.refs_24_ = bf16[64,2048]{1,0:T(8,128)(2,1)S(1)} collective-permute-done((bf16[64,2048]{1,0:T(8,128)(2,1)S(1)}, bf16[64,2048]{1,0:T(8,128)(2,1)S(1)}, u32[]{:S(2)}, u32[]{:S(2)}) %collective-permute-start.15) | collective-permute-done | bytes 262176 | tf_op jit(solution)/shard_map/ppermute | solution.py:253
  72.2 1.5 collective-permute-start.12
  74.4 3.1 %collective-permute-done.18.refs_22_ = bf16[64,2048]{1,0:T(8,128)(2,1)S(1)} collective-permute-done((bf16[64,2048]{1,0:T(8,128)(2,1)S(1)}, bf16[64,2048]{1,0:T(8,128)(2,1)S(1)}, u32[]{:S(2)}, u32[]{:S(2)}) %collective-permute-start.18) | collective-permute-done | bytes 262176 | tf_op jit(solution)/shard_map/ppermute | solution.py:42
  79.3 3.4 %collective-permute-start.14 = (bf16[3,64,2048]{2,1,0:T(8,128)(2,1)S(1)}, bf16[3,64,2048]{2,1,0:T(8,128)(2,1)S(1)}, u32[]{:S(2)}, u32[]{:S(2)}) collective-permute-start(bf16[3,64,2048]{2,1,0:T(8,128)(2,1)S(1)} %collective-permute-done.3), channel_id=1, source_target_pairs={{0,2},{2,6},{6,4},{4,0},{1,3},{3,7},{7,5},{5,1},{8,10},{10,14},{14... | collective-permute-start | bytes 2359304 | tf_op jit(solution)/shard_map/ppermute | solution.py:253
  83.6 5.0 %collective-permute-done.12.rest_3_ = bf16[128,2048]{1,0:T(8,128)(2,1)} collective-permute-done((bf16[128,2048]{1,0:T(8,128)(2,1)S(1)}, bf16[128,2048]{1,0:T(8,128)(2,1)}, u32[]{:S(2)}, u32[]{:S(2)}) %collective-permute-start.12) | collective-permute-done | bytes 524320 | tf_op jit(solution)/shard_map/ppermute | solution.py:42
  88.6 1.5 collective-permute-start.13
  90.1 11.4 %collective-permute-done.13.rest_4_ = bf16[128,2048]{1,0:T(8,128)(2,1)} collective-permute-done((bf16[128,2048]{1,0:T(8,128)(2,1)S(1)}, bf16[128,2048]{1,0:T(8,128)(2,1)}, u32[]{:S(2)}, u32[]{:S(2)}) %collective-permute-start.13) | collective-permute-done | bytes 524320 | tf_op jit(solution)/shard_map/ppermute | solution.py:42
  105.2 1.5 collective-permute-start.24
  106.7 3.4 %collective-permute-start.22 = (bf16[3,64,2048]{2,1,0:T(8,128)(2,1)}, bf16[3,64,2048]{2,1,0:T(8,128)(2,1)}, u32[]{:S(2)}, u32[]{:S(2)}) collective-permute-start(bf16[3,64,2048]{2,1,0:T(8,128)(2,1)} %copy-done.22), channel_id=1, source_target_pairs={{0,2},{2,6},{6,4},{4,0},{1,3},{3,7},{7,5},{5,1},{8,10},{10,14},{14... | collective-permute-start | bytes 2359304 | tf_op jit(solution)/shard_map/ppermute | solution.py:253
  115.7 1.5 pad.14.taps_ref
  119.7 1.5 collective-permute-start.25
  122.6 1.5 collective-permute-start.27
  124.7 1.2 copy-done.2
  126.0 1.2 copy-done.5
  127.2 1.2 copy-done.7
  128.4 1.1 copy-done.23
  130.4 10.8 %shard_map.66 = (bf16[64,512]{1,0:T(8,128)(2,1)S(1)}, bf16[64,512]{1,0:T(8,128)(2,1)S(1)}, bf16[64,512]{1,0:T(8,128)(2,1)S(1)}, bf16[64,512]{1,0:T(8,128)(2,1)S(1)}) custom-call(s32[1]{0:T(128)} %bitcast.core_ref, bf16[192,2048]{1,0:T(8,128)(2,1)S(1)} %bitcast.27, f32[192,8]{1,0:T(8,128)S(1)} %copy-done.26, f32[4,128]{1,0:T(4,128)S(1)} %get-tuple-element.136.long_ref, ...), custom_call_target="tpu_custom_call" | custom-call | flops 1610612736 | bytes 8388608 | tf_op jit(solution)/shard_map/pallas_call | solution.py:168
  142.3 10.8 %shard_map.65 = (bf16[64,512]{1,0:T(8,128)(2,1)S(1)}, bf16[64,512]{1,0:T(8,128)(2,1)S(1)}, bf16[64,512]{1,0:T(8,128)(2,1)S(1)}, bf16[64,512]{1,0:T(8,128)(2,1)S(1)}) custom-call(s32[1]{0:T(128)} %bitcast.core_ref, bf16[192,2048]{1,0:T(8,128)(2,1)S(1)} %bitcast.26, f32[192,8]{1,0:T(8,128)S(1)} %copy-done.25, f32[4,128]{1,0:T(4,128)S(1)} %get-tuple-element.134.long_ref, ...), custom_call_target="tpu_custom_call" | custom-call | flops 1610612736 | bytes 8388608 | tf_op jit(solution)/shard_map/pallas_call | solution.py:168
  153.1 1.2 collective-permute-start.42
  154.3 1.5 collective-permute-start.43
  156.6 10.7 %shard_map.64 = (bf16[64,512]{1,0:T(8,128)(2,1)S(1)}, bf16[64,512]{1,0:T(8,128)(2,1)S(1)}, bf16[64,512]{1,0:T(8,128)(2,1)S(1)}, bf16[64,512]{1,0:T(8,128)(2,1)S(1)}) custom-call(s32[1]{0:T(128)} %bitcast.core_ref, bf16[192,2048]{1,0:T(8,128)(2,1)S(1)} %bitcast.25, f32[192,8]{1,0:T(8,128)S(1)} %copy-done.24, f32[4,128]{1,0:T(4,128)S(1)} %get-tuple-element.135.long_ref, ...), custom_call_target="tpu_custom_call" | custom-call | flops 1610612736 | bytes 8388608 | tf_op jit(solution)/shard_map/pallas_call | solution.py:168
  167.4 11.8 %shard_map.67 = (bf16[64,512]{1,0:T(8,128)(2,1)S(1)}, bf16[64,512]{1,0:T(8,128)(2,1)S(1)}, bf16[64,512]{1,0:T(8,128)(2,1)S(1)}, bf16[64,512]{1,0:T(8,128)(2,1)S(1)}) custom-call(s32[1]{0:T(128)} %bitcast.core_ref, bf16[192,2048]{1,0:T(8,128)(2,1)} %bitcast.17.w_ref, f32[192,8]{1,0:T(8,128)S(1)} %pad.16.taps_ref, f32[4,128]{1,0:T(4,128)S(1)} %get-tuple-element.133.long_ref, ...), custom_call_target="tpu_custom_call" | custom-call | flops 1610612736 | bytes 8388608 | tf_op jit(solution)/shard_map/pallas_call | solution.py:168
  179.2 1.2 collective-permute-start.38
  180.4 1.5 collective-permute-start.39
  182.8 1.1 collective-permute-start.29
  183.9 1.5 collective-permute-start.30
  186.3 1.1 collective-permute-start.32
  187.4 1.5 collective-permute-start.33
  189.8 1.1 collective-permute-start.35
  190.9 1.5 collective-permute-start.36
  192.4 1.1 collective-permute-start.37
  194.0 1.1 collective-permute-done.36.refs_10_
  195.2 2.4 %collective-permute-done.37.refs_11_ = bf16[64,512]{1,0:T(8,128)(2,1)S(1)} collective-permute-done((bf16[64,512]{1,0:T(8,128)(2,1)S(1)}, bf16[64,512]{1,0:T(8,128)(2,1)S(1)}, u32[]{:S(2)}, u32[]{:S(2)}) %collective-permute-start.37) | collective-permute-done | bytes 65568 | tf_op jit(solution)/shard_map/ppermute | solution.py:42
  197.6 3.4 %shard_map.69 = bf16[256,2048]{1,0:T(8,128)(2,1)S(1)} custom-call(s32[1]{0:T(128)S(6)} %sub.20.core_ref, bf16[64,512]{1,0:T(8,128)(2,1)S(1)} %get-tuple-element.98.refs_0_, bf16[64,512]{1,0:T(8,128)(2,1)S(1)} %collective-permute-done.29.refs_1_, bf16[64,512]{1,0:T(8,128)(2,1)S(1)} %collective-permute-done.30.refs_2_, ...), custom_call_target="tpu_custom_call" | custom-call | flops 1073741824 | bytes 5242880 | tf_op jit(solution)/shard_map/pallas_call | solution.py:221
  201.1 3.4 %shard_map.68 = f32[256,2048]{1,0:T(8,128)S(1)} custom-call(s32[1]{0:T(128)} %bitcast.core_ref, bf16[64,512]{1,0:T(8,128)(2,1)S(1)} %get-tuple-element.98.refs_0_, bf16[64,512]{1,0:T(8,128)(2,1)S(1)} %collective-permute-done.29.refs_1_, bf16[64,512]{1,0:T(8,128)(2,1)S(1)} %collective-permute-done.30.refs_2_, ...), custom_call_target="tpu_custom_call" | custom-call | flops 1073741824 | bytes 5242880 | tf_op jit(solution)/shard_map/pallas_call | solution.py:221
  204.6 1.3 add_convert_fusion
  (128 shorter events, 24.4 us)
Async XLA Ops:
  1.2 1.4 collective-permute-start.5
  1.9 0.7 collective-permute-start.6
  2.7 13.8 %collective-permute-start.7 = (bf16[144,1024]{1,0:T(8,128)(2,1)S(1)}, bf16[144,1024]{1,0:T(8,128)(2,1)S(1)}, u32[]{:S(2)}, u32[]{:S(2)}) collective-permute-start(bf16[144,1024]{1,0:T(8,128)(2,1)S(1)} %add.70), channel_id=1, source_target_pairs={{0,8},{8,0},{16,24},{24,16},{1,9},{9,1},{17,25},{25,17},{2,10},{10... | collective-permute-start | bytes 884744 | tf_op jit(solution)/shard_map/ppermute | solution.py:42
  5.7 57.6 %collective-permute-start = (bf16[256,2048]{1,0:T(8,128)(2,1)S(1)}, bf16[256,2048]{1,0:T(8,128)(2,1)S(1)}, u32[]{:S(2)}, u32[]{:S(2)}) collective-permute-start(bf16[256,2048]{1,0:T(8,128)(2,1)S(1)} %copy-done), channel_id=1, source_target_pairs={{0,8},{8,0},{16,24},{24,16},{1,9},{9,1},{17,25},{25,17},{2,10},{10... | collective-permute-start | bytes 3145736 | tf_op jit(solution)/shard_map/ppermute | solution.py:42
  5.8 57.5 %collective-permute-start.1 = (bf16[256,2048]{1,0:T(8,128)(2,1)S(1)}, bf16[256,2048]{1,0:T(8,128)(2,1)S(1)}, u32[]{:S(2)}, u32[]{:S(2)}) collective-permute-start(bf16[256,2048]{1,0:T(8,128)(2,1)S(1)} %copy-done), channel_id=1, source_target_pairs={{0,16},{8,24},{16,0},{24,8},{1,17},{9,25},{17,1},{25,9},{2,18},{10... | collective-permute-start | bytes 3145736 | tf_op jit(solution)/shard_map/ppermute | solution.py:42
  7.7 55.6 %collective-permute-start.2 = (bf16[256,2048]{1,0:T(8,128)(2,1)S(1)}, bf16[256,2048]{1,0:T(8,128)(2,1)S(1)}, u32[]{:S(2)}, u32[]{:S(2)}) collective-permute-start(bf16[256,2048]{1,0:T(8,128)(2,1)S(1)} %copy-done), channel_id=1, source_target_pairs={{0,1},{1,0},{2,3},{3,2},{4,5},{5,4},{6,7},{7,6},{8,9},{9,8},{10,11... | collective-permute-start | bytes 3145736 | tf_op jit(solution)/shard_map/ppermute | solution.py:37
  16.0 14.1 %collective-permute-start.8 = (bf16[144,1024]{1,0:T(8,128)(2,1)S(1)}, bf16[144,1024]{1,0:T(8,128)(2,1)S(1)}, u32[]{:S(2)}, u32[]{:S(2)}) collective-permute-start(bf16[144,1024]{1,0:T(8,128)(2,1)S(1)} %add.70), channel_id=1, source_target_pairs={{0,16},{8,24},{16,0},{24,8},{1,17},{9,25},{17,1},{25,9},{2,18},{10... | collective-permute-start | bytes 884744 | tf_op jit(solution)/shard_map/ppermute | solution.py:42
  16.5 46.8 %collective-permute-start.3 = (bf16[3,64,2048]{2,1,0:T(8,128)(2,1)}, bf16[3,64,2048]{2,1,0:T(8,128)(2,1)S(1)}, u32[]{:S(2)}, u32[]{:S(2)}) collective-permute-start(bf16[3,64,2048]{2,1,0:T(8,128)(2,1)} %param.7), channel_id=1, source_target_pairs={{0,2},{2,6},{6,4},{4,0},{1,3},{3,7},{7,5},{5,1},{8,10},{10,14},{14... | collective-permute-start | bytes 2359304 | tf_op jit(solution)/shard_map/ppermute | solution.py:253
  30.1 10.7 %collective-permute-start.9 = (bf16[144,1024]{1,0:T(8,128)(2,1)S(1)}, bf16[144,1024]{1,0:T(8,128)(2,1)S(1)}, u32[]{:S(2)}, u32[]{:S(2)}) collective-permute-start(bf16[144,1024]{1,0:T(8,128)(2,1)S(1)} %add.70), channel_id=1, source_target_pairs={{0,24},{8,16},{16,8},{24,0},{1,25},{9,17},{17,9},{25,1},{2,26},{10... | collective-permute-start | bytes 884744 | tf_op jit(solution)/shard_map/ppermute | solution.py:42
  40.8 22.5 %collective-permute-start.4 = (bf16[64,2048]{1,0:T(8,128)(2,1)S(1)}, bf16[64,2048]{1,0:T(8,128)(2,1)S(1)}, u32[]{:S(2)}, u32[]{:S(2)}) collective-permute-start(bf16[64,2048]{1,0:T(8,128)(2,1)S(1)} %copy-done.8), channel_id=1, source_target_pairs={{0,2},{2,6},{6,4},{4,0},{1,3},{3,7},{7,5},{5,1},{8,10},{10,14},{14... | collective-permute-start | bytes 786440 | tf_op jit(solution)/shard_map/ppermute | solution.py:253
  55.8 48.3 %copy-start.27 = (bf16[4,144,1024]{2,1,0:T(8,128)(2,1)}, bf16[4,144,1024]{2,1,0:T(8,128)(2,1)S(1)}, u32[]{:S(2)}) copy-start(bf16[4,144,1024]{2,1,0:T(8,128)(2,1)S(1)} %pad_maximum_fusion.rest_10_) | copy-start | bytes 3538948
  55.8 49.3 %copy-start.29 = (s32[4,4]{1,0:T(4,128)S(1)}, s32[4,4]{1,0:T(4,128)}, u32[]{:S(2)}) copy-start(s32[4,4]{1,0:T(4,128)} %constant.68.clone) | copy-start | bytes 196
  63.4 8.8 %collective-permute-start.15 = (bf16[64,2048]{1,0:T(8,128)(2,1)S(1)}, bf16[64,2048]{1,0:T(8,128)(2,1)S(1)}, u32[]{:S(2)}, u32[]{:S(2)}) collective-permute-start(bf16[64,2048]{1,0:T(8,128)(2,1)S(1)} %collective-permute-done.4.refs_20_), channel_id=1, source_target_pairs={{0,2},{2,6},{6,4},{4,0},{1,3},{3,7},{7,5},{5,1},{8,10},{10,14},{14... | collective-permute-start | bytes 786440 | tf_op jit(solution)/shard_map/ppermute | solution.py:253
  64.3 9.3 %collective-permute-start.17 = (bf16[64,2048]{1,0:T(8,128)(2,1)S(1)}, bf16[64,2048]{1,0:T(8,128)(2,1)S(1)}, u32[]{:S(2)}, u32[]{:S(2)}) collective-permute-start(bf16[64,2048]{1,0:T(8,128)(2,1)S(1)} %collective-permute-done.4.refs_20_), channel_id=1, source_target_pairs={{0,8},{8,0},{16,24},{24,16},{1,9},{9,1},{17,25},{25,17},{2,10},{10... | collective-permute-start | bytes 786440 | tf_op jit(solution)/shard_map/ppermute | solution.py:42
  65.8 11.7 %collective-permute-start.18 = (bf16[64,2048]{1,0:T(8,128)(2,1)S(1)}, bf16[64,2048]{1,0:T(8,128)(2,1)S(1)}, u32[]{:S(2)}, u32[]{:S(2)}) collective-permute-start(bf16[64,2048]{1,0:T(8,128)(2,1)S(1)} %collective-permute-done.4.refs_20_), channel_id=1, source_target_pairs={{0,16},{8,24},{16,0},{24,8},{1,17},{9,25},{17,1},{25,9},{2,18},{10... | collective-permute-start | bytes 786440 | tf_op jit(solution)/shard_map/ppermute | solution.py:42
  67.3 36.2 %collective-permute-start.16 = (bf16[4,144,1024]{2,1,0:T(8,128)(2,1)S(1)}, bf16[4,144,1024]{2,1,0:T(8,128)(2,1)S(1)}, u32[]{:S(2)}, u32[]{:S(2)}) collective-permute-start(bf16[4,144,1024]{2,1,0:T(8,128)(2,1)S(1)} %pad_maximum_fusion.rest_10_), channel_id=1, source_target_pairs={{0,1},{1,0},{2,3},{3,2},{4,5},{5,4},{6,7},{7,6},{8,9},{9,8},{10,11... | collective-permute-start | bytes 3538952 | tf_op jit(solution)/shard_map/ppermute | solution.py:37
  67.3 11.9 %collective-permute-start.19 = (bf16[64,2048]{1,0:T(8,128)(2,1)S(1)}, bf16[64,2048]{1,0:T(8,128)(2,1)S(1)}, u32[]{:S(2)}, u32[]{:S(2)}) collective-permute-start(bf16[64,2048]{1,0:T(8,128)(2,1)S(1)} %collective-permute-done.4.refs_20_), channel_id=1, source_target_pairs={{0,24},{8,16},{16,8},{24,0},{1,25},{9,17},{17,9},{25,1},{2,26},{10... | collective-permute-start | bytes 786440 | tf_op jit(solution)/shard_map/ppermute | solution.py:42
  72.2 16.4 %collective-permute-start.12 = (bf16[128,2048]{1,0:T(8,128)(2,1)S(1)}, bf16[128,2048]{1,0:T(8,128)(2,1)}, u32[]{:S(2)}, u32[]{:S(2)}) collective-permute-start(bf16[128,2048]{1,0:T(8,128)(2,1)S(1)} %slice.33), channel_id=1, source_target_pairs={{0,8},{8,0},{16,24},{24,16},{1,9},{9,1},{17,25},{25,17},{2,10},{10... | collective-permute-start | bytes 1572872 | tf_op jit(solution)/shard_map/ppermute | solution.py:42
  74.4 27.1 %collective-permute-start.10 = (bf16[256,2048]{1,0:T(8,128)(2,1)S(1)}, bf16[256,2048]{1,0:T(8,128)(2,1)S(1)}, u32[]{:S(2)}, u32[]{:S(2)}) collective-permute-start(bf16[256,2048]{1,0:T(8,128)(2,1)S(1)} %collective-permute-done.rest_1_), channel_id=1, source_target_pairs={{0,1},{1,0},{2,3},{3,2},{4,5},{5,4},{6,7},{7,6},{8,9},{9,8},{10,11... | collective-permute-start | bytes 3145736 | tf_op jit(solution)/shard_map/ppermute | solution.py:37
  78.2 24.3 %collective-permute-start.11 = (bf16[256,2048]{1,0:T(8,128)(2,1)S(1)}, bf16[256,2048]{1,0:T(8,128)(2,1)S(1)}, u32[]{:S(2)}, u32[]{:S(2)}) collective-permute-start(bf16[256,2048]{1,0:T(8,128)(2,1)S(1)} %collective-permute-done.1.rest_2_), channel_id=1, source_target_pairs={{0,1},{1,0},{2,3},{3,2},{4,5},{5,4},{6,7},{7,6},{8,9},{9,8},{10,11... | collective-permute-start | bytes 3145736 | tf_op jit(solution)/shard_map/ppermute | solution.py:37
  79.3 22.3 %collective-permute-start.14 = (bf16[3,64,2048]{2,1,0:T(8,128)(2,1)S(1)}, bf16[3,64,2048]{2,1,0:T(8,128)(2,1)S(1)}, u32[]{:S(2)}, u32[]{:S(2)}) collective-permute-start(bf16[3,64,2048]{2,1,0:T(8,128)(2,1)S(1)} %collective-permute-done.3), channel_id=1, source_target_pairs={{0,2},{2,6},{6,4},{4,0},{1,3},{3,7},{7,5},{5,1},{8,10},{10,14},{14... | collective-permute-start | bytes 2359304 | tf_op jit(solution)/shard_map/ppermute | solution.py:253
  88.6 13.0 %collective-permute-start.13 = (bf16[128,2048]{1,0:T(8,128)(2,1)S(1)}, bf16[128,2048]{1,0:T(8,128)(2,1)}, u32[]{:S(2)}, u32[]{:S(2)}) collective-permute-start(bf16[128,2048]{1,0:T(8,128)(2,1)S(1)} %slice.34), channel_id=1, source_target_pairs={{0,16},{8,24},{16,0},{24,8},{1,17},{9,25},{17,1},{25,9},{2,18},{10... | collective-permute-start | bytes 1572872 | tf_op jit(solution)/shard_map/ppermute | solution.py:42
  103.6 19.0 %collective-permute-start.20 = (bf16[128,2048]{1,0:T(8,128)(2,1)}, bf16[128,2048]{1,0:T(8,128)(2,1)}, u32[]{:S(2)}, u32[]{:S(2)}) collective-permute-start(bf16[128,2048]{1,0:T(8,128)(2,1)} %collective-permute-done.12.rest_3_), channel_id=1, source_target_pairs={{0,1},{1,0},{2,3},{3,2},{4,5},{5,4},{6,7},{7,6},{8,9},{9,8},{10,11... | collective-permute-start | bytes 1572872 | tf_op jit(solution)/shard_map/ppermute | solution.py:37
  103.7 20.4 %collective-permute-start.21 = (bf16[128,2048]{1,0:T(8,128)(2,1)}, bf16[128,2048]{1,0:T(8,128)(2,1)}, u32[]{:S(2)}, u32[]{:S(2)}) collective-permute-start(bf16[128,2048]{1,0:T(8,128)(2,1)} %collective-permute-done.13.rest_4_), channel_id=1, source_target_pairs={{0,1},{1,0},{2,3},{3,2},{4,5},{5,4},{6,7},{7,6},{8,9},{9,8},{10,11... | collective-permute-start | bytes 1572872 | tf_op jit(solution)/shard_map/ppermute | solution.py:37
  104.6 15.1 %collective-permute-start.23 = (bf16[64,2048]{1,0:T(8,128)(2,1)S(1)}, bf16[64,2048]{1,0:T(8,128)(2,1)}, u32[]{:S(2)}, u32[]{:S(2)}) collective-permute-start(bf16[64,2048]{1,0:T(8,128)(2,1)S(1)} %copy-done.8), channel_id=1, source_target_pairs={{0,8},{8,0},{16,24},{24,16},{1,9},{9,1},{17,25},{25,17},{2,10},{10... | collective-permute-start | bytes 786440 | tf_op jit(solution)/shard_map/ppermute | solution.py:42
  105.2 16.8 %collective-permute-start.24 = (bf16[64,2048]{1,0:T(8,128)(2,1)S(1)}, bf16[64,2048]{1,0:T(8,128)(2,1)}, u32[]{:S(2)}, u32[]{:S(2)}) collective-permute-start(bf16[64,2048]{1,0:T(8,128)(2,1)S(1)} %copy-done.8), channel_id=1, source_target_pairs={{0,16},{8,24},{16,0},{24,8},{1,17},{9,25},{17,1},{25,9},{2,18},{10... | collective-permute-start | bytes 786440 | tf_op jit(solution)/shard_map/ppermute | solution.py:42
  106.7 60.6 %collective-permute-start.22 = (bf16[3,64,2048]{2,1,0:T(8,128)(2,1)}, bf16[3,64,2048]{2,1,0:T(8,128)(2,1)}, u32[]{:S(2)}, u32[]{:S(2)}) collective-permute-start(bf16[3,64,2048]{2,1,0:T(8,128)(2,1)} %copy-done.22), channel_id=1, source_target_pairs={{0,2},{2,6},{6,4},{4,0},{1,3},{3,7},{7,5},{5,1},{8,10},{10,14},{14... | collective-permute-start | bytes 2359304 | tf_op jit(solution)/shard_map/ppermute | solution.py:253
  119.7 21.6 %collective-permute-start.25 = (bf16[64,2048]{1,0:T(8,128)(2,1)S(1)}, bf16[64,2048]{1,0:T(8,128)(2,1)S(1)}, u32[]{:S(2)}, u32[]{:S(2)}) collective-permute-start(bf16[64,2048]{1,0:T(8,128)(2,1)S(1)} %copy-done.8), channel_id=1, source_target_pairs={{0,24},{8,16},{16,8},{24,0},{1,25},{9,17},{17,9},{25,1},{2,26},{10... | collective-permute-start | bytes 786440 | tf_op jit(solution)/shard_map/ppermute | solution.py:42
  122.0 32.3 %collective-permute-start.26 = (bf16[64,2048]{1,0:T(8,128)(2,1)}, bf16[64,2048]{1,0:T(8,128)(2,1)S(1)}, u32[]{:S(2)}, u32[]{:S(2)}) collective-permute-start(bf16[64,2048]{1,0:T(8,128)(2,1)} %copy-done.11), channel_id=1, source_target_pairs={{0,8},{8,0},{16,24},{24,16},{1,9},{9,1},{17,25},{25,17},{2,10},{10... | collective-permute-start | bytes 786440 | tf_op jit(solution)/shard_map/ppermute | solution.py:42
  122.6 33.1 %collective-permute-start.27 = (bf16[64,2048]{1,0:T(8,128)(2,1)}, bf16[64,2048]{1,0:T(8,128)(2,1)S(1)}, u32[]{:S(2)}, u32[]{:S(2)}) collective-permute-start(bf16[64,2048]{1,0:T(8,128)(2,1)} %copy-done.11), channel_id=1, source_target_pairs={{0,16},{8,24},{16,0},{24,8},{1,17},{9,25},{17,1},{25,9},{2,18},{10... | collective-permute-start | bytes 786440 | tf_op jit(solution)/shard_map/ppermute | solution.py:42
  124.1 29.0 %collective-permute-start.41 = (bf16[64,2048]{1,0:T(8,128)(2,1)}, bf16[64,2048]{1,0:T(8,128)(2,1)S(1)}, u32[]{:S(2)}, u32[]{:S(2)}) collective-permute-start(bf16[64,2048]{1,0:T(8,128)(2,1)} %copy-done.11), channel_id=1, source_target_pairs={{0,2},{2,6},{6,4},{4,0},{1,3},{3,7},{7,5},{5,1},{8,10},{10,14},{14... | collective-permute-start | bytes 786440 | tf_op jit(solution)/shard_map/ppermute | solution.py:253
  141.3 26.0 %collective-permute-start.28 = (bf16[64,2048]{1,0:T(8,128)(2,1)S(1)}, bf16[64,2048]{1,0:T(8,128)(2,1)S(1)}, u32[]{:S(2)}, u32[]{:S(2)}) collective-permute-start(bf16[64,2048]{1,0:T(8,128)(2,1)S(1)} %copy-done.12), channel_id=1, source_target_pairs={{0,24},{8,16},{16,8},{24,0},{1,25},{9,17},{17,9},{25,1},{2,26},{10... | collective-permute-start | bytes 786440 | tf_op jit(solution)/shard_map/ppermute | solution.py:42
  153.1 28.8 %collective-permute-start.42 = (bf16[64,2048]{1,0:T(8,128)(2,1)S(1)}, bf16[64,2048]{1,0:T(8,128)(2,1)S(1)}, u32[]{:S(2)}, u32[]{:S(2)}) collective-permute-start(bf16[64,2048]{1,0:T(8,128)(2,1)S(1)} %collective-permute-done.41.refs_28_), channel_id=1, source_target_pairs={{0,8},{8,0},{16,24},{24,16},{1,9},{9,1},{17,25},{25,17},{2,10},{10... | collective-permute-start | bytes 786440 | tf_op jit(solution)/shard_map/ppermute | solution.py:42
  154.3 28.5 %collective-permute-start.43 = (bf16[64,2048]{1,0:T(8,128)(2,1)S(1)}, bf16[64,2048]{1,0:T(8,128)(2,1)S(1)}, u32[]{:S(2)}, u32[]{:S(2)}) collective-permute-start(bf16[64,2048]{1,0:T(8,128)(2,1)S(1)} %collective-permute-done.41.refs_28_), channel_id=1, source_target_pairs={{0,16},{8,24},{16,0},{24,8},{1,17},{9,25},{17,1},{25,9},{2,18},{10... | collective-permute-start | bytes 786440 | tf_op jit(solution)/shard_map/ppermute | solution.py:42
  155.7 28.2 %collective-permute-start.44 = (bf16[64,2048]{1,0:T(8,128)(2,1)S(1)}, bf16[64,2048]{1,0:T(8,128)(2,1)S(1)}, u32[]{:S(2)}, u32[]{:S(2)}) collective-permute-start(bf16[64,2048]{1,0:T(8,128)(2,1)S(1)} %collective-permute-done.41.refs_28_), channel_id=1, source_target_pairs={{0,24},{8,16},{16,8},{24,0},{1,25},{9,17},{17,9},{25,1},{2,26},{10... | collective-permute-start | bytes 786440 | tf_op jit(solution)/shard_map/ppermute | solution.py:42
  179.2 6.2 %collective-permute-start.38 = (bf16[64,512]{1,0:T(8,128)(2,1)S(1)}, bf16[64,512]{1,0:T(8,128)(2,1)S(1)}, u32[]{:S(2)}, u32[]{:S(2)}) collective-permute-start(bf16[64,512]{1,0:T(8,128)(2,1)S(1)} %get-tuple-element.112), channel_id=1, source_target_pairs={{0,8},{8,0},{16,24},{24,16},{1,9},{9,1},{17,25},{25,17},{2,10},{10... | collective-permute-start | bytes 196616 | tf_op jit(solution)/shard_map/ppermute | solution.py:42
  180.4 5.9 %collective-permute-start.39 = (bf16[64,512]{1,0:T(8,128)(2,1)S(1)}, bf16[64,512]{1,0:T(8,128)(2,1)S(1)}, u32[]{:S(2)}, u32[]{:S(2)}) collective-permute-start(bf16[64,512]{1,0:T(8,128)(2,1)S(1)} %get-tuple-element.113), channel_id=1, source_target_pairs={{0,16},{8,24},{16,0},{24,8},{1,17},{9,25},{17,1},{25,9},{2,18},{10... | collective-permute-start | bytes 196616 | tf_op jit(solution)/shard_map/ppermute | solution.py:42
  181.9 5.5 %collective-permute-start.40 = (bf16[64,512]{1,0:T(8,128)(2,1)S(1)}, bf16[64,512]{1,0:T(8,128)(2,1)S(1)}, u32[]{:S(2)}, u32[]{:S(2)}) collective-permute-start(bf16[64,512]{1,0:T(8,128)(2,1)S(1)} %get-tuple-element.114), channel_id=1, source_target_pairs={{0,24},{8,16},{16,8},{24,0},{1,25},{9,17},{17,9},{25,1},{2,26},{10... | collective-permute-start | bytes 196616 | tf_op jit(solution)/shard_map/ppermute | solution.py:42
  182.8 6.1 %collective-permute-start.29 = (bf16[64,512]{1,0:T(8,128)(2,1)S(1)}, bf16[64,512]{1,0:T(8,128)(2,1)S(1)}, u32[]{:S(2)}, u32[]{:S(2)}) collective-permute-start(bf16[64,512]{1,0:T(8,128)(2,1)S(1)} %get-tuple-element.99), channel_id=1, source_target_pairs={{0,8},{8,0},{16,24},{24,16},{1,9},{9,1},{17,25},{25,17},{2,10},{10... | collective-permute-start | bytes 196616 | tf_op jit(solution)/shard_map/ppermute | solution.py:42
  183.9 5.9 %collective-permute-start.30 = (bf16[64,512]{1,0:T(8,128)(2,1)S(1)}, bf16[64,512]{1,0:T(8,128)(2,1)S(1)}, u32[]{:S(2)}, u32[]{:S(2)}) collective-permute-start(bf16[64,512]{1,0:T(8,128)(2,1)S(1)} %get-tuple-element.100), channel_id=1, source_target_pairs={{0,16},{8,24},{16,0},{24,8},{1,17},{9,25},{17,1},{25,9},{2,18},{10... | collective-permute-start | bytes 196616 | tf_op jit(solution)/shard_map/ppermute | solution.py:42
  185.4 5.5 %collective-permute-start.31 = (bf16[64,512]{1,0:T(8,128)(2,1)S(1)}, bf16[64,512]{1,0:T(8,128)(2,1)S(1)}, u32[]{:S(2)}, u32[]{:S(2)}) collective-permute-start(bf16[64,512]{1,0:T(8,128)(2,1)S(1)} %get-tuple-element.101), channel_id=1, source_target_pairs={{0,24},{8,16},{16,8},{24,0},{1,25},{9,17},{17,9},{25,1},{2,26},{10... | collective-permute-start | bytes 196616 | tf_op jit(solution)/shard_map/ppermute | solution.py:42
  186.3 6.1 %collective-permute-start.32 = (bf16[64,512]{1,0:T(8,128)(2,1)S(1)}, bf16[64,512]{1,0:T(8,128)(2,1)S(1)}, u32[]{:S(2)}, u32[]{:S(2)}) collective-permute-start(bf16[64,512]{1,0:T(8,128)(2,1)S(1)} %get-tuple-element.103), channel_id=1, source_target_pairs={{0,8},{8,0},{16,24},{24,16},{1,9},{9,1},{17,25},{25,17},{2,10},{10... | collective-permute-start | bytes 196616 | tf_op jit(solution)/shard_map/ppermute | solution.py:42
  187.4 6.0 %collective-permute-start.33 = (bf16[64,512]{1,0:T(8,128)(2,1)S(1)}, bf16[64,512]{1,0:T(8,128)(2,1)S(1)}, u32[]{:S(2)}, u32[]{:S(2)}) collective-permute-start(bf16[64,512]{1,0:T(8,128)(2,1)S(1)} %get-tuple-element.104), channel_id=1, source_target_pairs={{0,16},{8,24},{16,0},{24,8},{1,17},{9,25},{17,1},{25,9},{2,18},{10... | collective-permute-start | bytes 196616 | tf_op jit(solution)/shard_map/ppermute | solution.py:42
  188.9 5.2 %collective-permute-start.34 = (bf16[64,512]{1,0:T(8,128)(2,1)S(1)}, bf16[64,512]{1,0:T(8,128)(2,1)S(1)}, u32[]{:S(2)}, u32[]{:S(2)}) collective-permute-start(bf16[64,512]{1,0:T(8,128)(2,1)S(1)} %get-tuple-element.105), channel_id=1, source_target_pairs={{0,24},{8,16},{16,8},{24,0},{1,25},{9,17},{17,9},{25,1},{2,26},{10... | collective-permute-start | bytes 196616 | tf_op jit(solution)/shard_map/ppermute | solution.py:42
  189.8 4.3 %collective-permute-start.35 = (bf16[64,512]{1,0:T(8,128)(2,1)S(1)}, bf16[64,512]{1,0:T(8,128)(2,1)S(1)}, u32[]{:S(2)}, u32[]{:S(2)}) collective-permute-start(bf16[64,512]{1,0:T(8,128)(2,1)S(1)} %get-tuple-element.107), channel_id=1, source_target_pairs={{0,8},{8,0},{16,24},{24,16},{1,9},{9,1},{17,25},{25,17},{2,10},{10... | collective-permute-start | bytes 196616 | tf_op jit(solution)/shard_map/ppermute | solution.py:42
  190.9 4.3 %collective-permute-start.36 = (bf16[64,512]{1,0:T(8,128)(2,1)S(1)}, bf16[64,512]{1,0:T(8,128)(2,1)S(1)}, u32[]{:S(2)}, u32[]{:S(2)}) collective-permute-start(bf16[64,512]{1,0:T(8,128)(2,1)S(1)} %get-tuple-element.108), channel_id=1, source_target_pairs={{0,16},{8,24},{16,0},{24,8},{1,17},{9,25},{17,1},{25,9},{2,18},{10... | collective-permute-start | bytes 196616 | tf_op jit(solution)/shard_map/ppermute | solution.py:42
  192.4 5.2 %collective-permute-start.37 = (bf16[64,512]{1,0:T(8,128)(2,1)S(1)}, bf16[64,512]{1,0:T(8,128)(2,1)S(1)}, u32[]{:S(2)}, u32[]{:S(2)}) collective-permute-start(bf16[64,512]{1,0:T(8,128)(2,1)S(1)} %get-tuple-element.109), channel_id=1, source_target_pairs={{0,24},{8,16},{16,8},{24,0},{1,25},{9,17},{17,9},{25,1},{2,26},{10... | collective-permute-start | bytes 196616 | tf_op jit(solution)/shard_map/ppermute | solution.py:42
  201.0 3.5 %collective-permute-start.45 = (bf16[256,2048]{1,0:T(8,128)(2,1)S(1)}, bf16[256,2048]{1,0:T(8,128)(2,1)S(1)}, u32[]{:S(2)}, u32[]{:S(2)}) collective-permute-start(bf16[256,2048]{1,0:T(8,128)(2,1)S(1)} %shard_map.69), channel_id=1, source_target_pairs={{0,1},{1,0},{2,3},{3,2},{4,5},{5,4},{6,7},{7,6},{8,9},{9,8},{10,11... | collective-permute-start | bytes 3145736 | tf_op jit(solution)/shard_map/ppermute | solution.py:37
  (28 other events, 364.0 us)
where the time goes:
time: 206 us
  starting transfers between devices  76.9 us (37%)
  waiting for transfers between devices  53.8 us (26%)
  Pallas kernels  51 us (25%)
  local copies, waits for them, and re-layouts  18.8 us (9%)
  between operations  3.03 us (1%)
  other arithmetic  2.28 us (1%)
    pallas_call x4, Pallas kernels, mix_chunk(): pl.pallas_call(functools.partial(mix_kernel, places, slots), out_shape=[j...  44.1 us
    ppermute x31, waiting for transfers between devices, across(): return lax.ppermute(block, 'dp', [(i, i ^ r) for i in range(count)])  42 us
    ppermute x31, starting transfers between devices, across(): return lax.ppermute(block, 'dp', [(i, i ^ r) for i in range(count)])  39.8 us
    ppermute x6, starting transfers between devices, shards(): forward = lambda block: lax.ppermute(block, 'z', ring)  26.9 us
    ppermute x6, waiting for transfers between devices, shards(): forward = lambda block: lax.ppermute(block, 'z', ring)  11.8 us
    unnamed x60, local copies, waits for them, and re-layouts  10.5 us
    ppermute x7, starting transfers between devices, swap(): return lax.ppermute(block, 'core', [(0, 1), (1, 0)])  8.88 us
    pallas_call x2, Pallas kernels, project(): pl.pallas_call(functools.partial(out_kernel, count), out_shape=jax.ShapeD...  6.89 us
  transfers between devices with their start and end apart: 46, of which 11 were waited for; matrix products, arithmetic and copies ran while one was open for 4% of the time, Pallas kernels for 23%

commit v1 on v0

v1 whole, which is shorter than its diff:
```python
import functools

import jax
import jax.numpy as jnp
from jax import lax
from jax.experimental import pallas as pl
from jax.experimental.pallas import tpu as pltpu
from jax.sharding import Mesh
from jax.sharding import PartitionSpec as P

GSIZE = 16
SHORT = 7
TAPS = 128
EDGE = 144
LANES = 128
WIDE = 64
ANY = pl.BlockSpec(memory_space=pl.ANY)
SMEM = pl.BlockSpec(memory_space=pltpu.SMEM)
VMEM = pl.BlockSpec(memory_space=pltpu.VMEM)


def ring_of(count):
    order = [i for i in range(count) if i == 0 or i % 2 == 1]
    order += [i for i in reversed(range(1, count)) if i % 2 == 0]
    return [(order[i], order[(i + 1) % count]) for i in range(count)]


def origins_of(count):
    previous = dict((target, source) for source, target in ring_of(count))
    table = [list(range(count))]
    for _ in range(count - 1):
        table.append([previous[i] for i in table[-1]])
    return table


def swap(block):
    return lax.ppermute(block, "core", [(0, 1), (1, 0)])


def across(block, r):
    count = lax.axis_size("dp")
    return lax.ppermute(block, "dp", [(i, i ^ r) for i in range(count)])


def tn(a, b):
    return lax.dot_general(a, b, (((0,), (0,)), ((), ())), preferred_element_type=jnp.float32)


def rounded(x):
    return x.astype(jnp.bfloat16).astype(jnp.float32)


def dot(a, b):
    return jnp.dot(a, b, preferred_element_type=jnp.float32)


def mix_kernel(step, slots, place_ref, w_ref, taps_ref, long_ref, *rest):
    own_ref, sib_ref, near_ref, far_ref = rest[:4]
    outs, rest = rest[4 : 4 + slots], rest[4 + slots :]
    tokens, edges, wide_w, streams, query, gated, tiles, mixed, sems = rest
    rows = tokens.shape[2]
    half = edges.shape[3]
    core = place_ref[0]
    origin = place_ref[2 + step]
    count = WIDE // GSIZE

    copies = []
    for slot in range(slots):
        copies.append(
            [
                pltpu.make_async_copy(ref.at[at], dst.at[slot, side], sems.at[slot, n])
                for n, (ref, dst, side, at) in enumerate(
                    [
                        (near_ref, edges, 0, slot),
                        (far_ref, edges, 1, slot),
                        (own_ref, tokens, 0, lax.bitwise_xor(place_ref[1], slot)),
                        (sib_ref, tokens, 1, lax.bitwise_xor(place_ref[1], slot)),
                    ]
                )
            ]
        )
    for group in copies:
        for copy in group:
            copy.start()

    w = w_ref[...]
    pad = jnp.zeros((WIDE, w.shape[1]), w.dtype)
    wide_w[...] = jnp.concatenate([w[: 2 * WIDE], pad, w[2 * WIDE :]], axis=0).T
    filters = long_ref[origin]
    for g in range(count):
        line = jnp.concatenate([jnp.zeros((1, TAPS), jnp.float32), filters[g : g + 1, :]], axis=1)
        square = pltpu.roll(
            jnp.broadcast_to(line, (2 * TAPS, 2 * TAPS)), 0, 1, stride=1, stride_axis=0
        )
        tiles[g] = square[:, :TAPS].astype(jnp.bfloat16)
    taps = taps_ref[origin]

    blocks = 2 * rows // TAPS
    mine = pl.multiple_of(EDGE + core * rows, 16)
    theirs = pl.multiple_of(EDGE + (1 - core) * rows, 16)
    w_mine = pl.ds(pl.multiple_of(core * half, LANES), half)
    w_theirs = pl.ds(pl.multiple_of((1 - core) * half, LANES), half)
    band = 64

    def feat(at, lanes):
        total = None
        for j in range(SHORT):
            term = taps[j : j + 1, lanes] * streams[at - j : at - j + band, lanes]
            total = term if total is None else total + term
        return total

    def one(slot, carry):
        for k in range(slots):

            @pl.when(slot == k)
            def _():
                for copy in copies[k]:
                    copy.wait()

        streams[:EDGE, :] = rounded(
            dot(edges[slot, 0], wide_w[w_mine, :]) + dot(edges[slot, 1], wide_w[w_theirs, :])
        )
        streams[pl.ds(mine, rows), :] = rounded(dot(tokens[slot, 0], wide_w[...]))
        streams[pl.ds(theirs, rows), :] = rounded(dot(tokens[slot, 1], wide_w[...]))
        for at in range(EDGE - TAPS, EDGE + 2 * rows, band):
            first = feat(at, slice(0, LANES))
            second = feat(at, slice(LANES, 2 * LANES))
            here = at - (EDGE - TAPS)
            gated[here : here + band, :] = (first * second).astype(jnp.bfloat16)
            if at >= EDGE:
                query[at - EDGE : at - EDGE + band, :] = first
        turned = gated[...].T
        queries = query[...].T
        for g in range(count):
            part = turned[WIDE + g * GSIZE : WIDE + (g + 1) * GSIZE, :]
            window = jnp.concatenate(
                [part[:, b * TAPS : b * TAPS + 2 * TAPS] for b in range(blocks)], axis=0
            )
            conv = dot(window, tiles[g])
            row = jnp.concatenate(
                [conv[b * GSIZE : (b + 1) * GSIZE] for b in range(blocks)], axis=1
            )
            mixed[g * GSIZE : (g + 1) * GSIZE, :] = (
                queries[g * GSIZE : (g + 1) * GSIZE, :] * row
            ).astype(jnp.bfloat16)
        for k in range(slots):

            @pl.when(slot == k)
            def _():
                outs[k][...] = mixed[...]

        return carry

    lax.fori_loop(0, slots, one, 0)


def mix_chunk(step, place, w, taps, filters, own, sib, near, far):
    features = w.shape[1]
    slots, rows, _ = own.shape
    half = near.shape[2]
    count = WIDE // GSIZE
    return pl.pallas_call(
        functools.partial(mix_kernel, step, slots),
        out_shape=[jax.ShapeDtypeStruct((WIDE, 2 * rows), jnp.bfloat16)] * slots,
        in_specs=[SMEM, VMEM, VMEM, VMEM] + [ANY] * 4,
        out_specs=[VMEM] * slots,
        scratch_shapes=[
            pltpu.VMEM((slots, 2, rows, features), jnp.bfloat16),
            pltpu.VMEM((slots, 2, EDGE, half), jnp.bfloat16),
            pltpu.VMEM((features, 4 * WIDE), jnp.bfloat16),
            pltpu.VMEM((EDGE + 2 * rows, 4 * WIDE), jnp.float32),
            pltpu.VMEM((2 * rows, LANES), jnp.float32),
            pltpu.VMEM((TAPS + 2 * rows, LANES), jnp.bfloat16),
            pltpu.VMEM((count, 2 * TAPS, TAPS), jnp.bfloat16),
            pltpu.VMEM((WIDE, 2 * rows), jnp.bfloat16),
            pltpu.SemaphoreType.DMA((slots, 4)),
        ],
        compiler_params=pltpu.CompilerParams(vmem_limit_bytes=44 * 1024 * 1024),
        cost_estimate=pl.CostEstimate(
            flops=4 * slots * 2 * rows * 4 * WIDE * features,
            bytes_accessed=2 * slots * 2 * rows * features,
            transcendentals=0,
        ),
    )(place, w, taps, filters, own, sib, near, far)


def out_kernel(counts, core_ref, *refs):
    parts, refs = refs[: counts[0]], refs[counts[0] :]
    weights, refs = refs[: counts[1]], refs[counts[1] :]
    out_ref, left, right, sems = refs
    rows = out_ref.shape[0]
    copies = []
    for kind, (group, whole) in enumerate(((parts, left), (weights, right))):
        at = 0
        for n, ref in enumerate(group):
            here = pl.ds(at, ref.shape[0])
            copies.append(pltpu.make_async_copy(ref, whole.at[here], sems.at[kind, n]))
            at += ref.shape[0]
    for copy in copies:
        copy.start()
    for copy in copies:
        copy.wait()
    at = pl.multiple_of(core_ref[0] * rows, LANES)
    a = left[:, pl.ds(at, rows)].T
    tile = 512
    for t in range(0, out_ref.shape[1], tile):
        out_ref[:, t : t + tile] = dot(a, right[:, t : t + tile]).astype(out_ref.dtype)


def project(which, parts, weights, dtype):
    counts = (len(parts), len(weights))
    depth = sum(w.shape[0] for w in weights)
    span, width = parts[0].shape[1], weights[0].shape[1]
    rows = span // 2
    return pl.pallas_call(
        functools.partial(out_kernel, counts),
        out_shape=jax.ShapeDtypeStruct((rows, width), dtype),
        in_specs=[SMEM] + [ANY] * sum(counts),
        out_specs=VMEM,
        scratch_shapes=[
            pltpu.VMEM((depth, span), jnp.bfloat16),
            pltpu.VMEM((depth, width), jnp.bfloat16),
            pltpu.SemaphoreType.DMA((2, max(counts))),
        ],
        compiler_params=pltpu.CompilerParams(vmem_limit_bytes=44 * 1024 * 1024),
        cost_estimate=pl.CostEstimate(
            flops=4 * rows * width * depth,
            bytes_accessed=2 * depth * (width + span),
            transcendentals=0,
        ),
    )(which, *parts, *weights)


def tie(*groups):
    return lax.optimization_barrier(groups)


def shards(chips, tokens, in_weight, short_taps, long_taps, out_weight):
    _, width, features = in_weight.shape
    rows = tokens.shape[0]
    half = features // 2
    slots = lax.axis_size("dp")
    dp = lax.axis_index("dp")
    z = lax.axis_index("z")
    core = lax.axis_index("core")
    ring = ring_of(chips)
    forward = lambda block: lax.ppermute(block, "z", ring)

    table = jnp.array(origins_of(chips), jnp.int32)
    origins = lax.dynamic_index_in_dim(table, z, 1, False)
    place = jnp.concatenate([jnp.stack([core, dp]).astype(jnp.int32), origins])
    first = dp * chips * 2
    part = short_taps.reshape(SHORT, 3, -1, 2, width)
    part = lax.dynamic_slice(
        part, (0, 0, dp * chips, core, 0), (SHORT, 3, chips, 1, width)
    ).reshape(SHORT, 3, chips, width)
    part = jnp.pad(part, ((0, 1), (0, 0), (0, 0), (0, WIDE - width)))
    part = jnp.transpose(part, (2, 0, 1, 3))
    taps = jnp.concatenate(
        [part[:, :, 0], part[:, :, 1], jnp.zeros_like(part[:, :, 0]), part[:, :, 2]], axis=2
    )
    groups = max(1, width // GSIZE)
    each = jnp.stack(
        [
            lax.dynamic_slice_in_dim(
                long_taps, (first + 2 * i + core) * width // GSIZE, groups, 0
            )
            for i in range(chips)
        ]
    ).astype(jnp.float32)
    filters = jnp.pad(each, ((0, 0), (0, WIDE // GSIZE - groups), (0, 0)))

    own = lax.all_gather(tokens, "dp")
    pairs = lambda c: [(2 * i + 1, 2 * (i + 1) + c) for i in range(chips - 1)]
    last = tokens[rows - EDGE :]
    edge = lax.ppermute(last[:, :half], ("z", "core"), pairs(0)) + lax.ppermute(
        last[:, half:], ("z", "core"), pairs(1)
    )
    near = jnp.stack([edge] + [across(edge, r) for r in range(1, slots)])
    far = swap(near)

    ws, vs = [in_weight], [out_weight]
    for s in range(1, chips):
        ws.append(forward(ws[-1]))
        vs.append(forward(vs[-1]))
    every_v = jnp.concatenate(vs)

    own, far, every_v, ws[chips - 2] = tie(own, far, every_v, ws[chips - 2])
    if chips > 3:
        ws[chips - 1] = forward(ws[chips - 2])
    sib = swap(own)
    if slots == 4:
        v_x, v_y = across(every_v, 1), across(every_v, 2)
        cut = every_v.shape[0] // 2
        wide = [every_v, v_x, v_y, (across(v_y[:cut], 1), across(v_x[cut:], 2))]
    else:
        wide = [every_v] + [across(every_v, r) for r in range(1, slots)]
    lists = []
    for s in range(chips):
        w = ws[s]
        if width < WIDE:
            w = jnp.pad(w, ((0, 0), (0, WIDE - width), (0, 0)))
        mixed = mix_chunk(
            s, place, w.reshape(3 * WIDE, features), taps, filters, own, sib, near, far
        )
        mixed = [m[:width] for m in mixed]
        lists.append([mixed[0]] + [across(mixed[r], r) for r in range(1, slots)])
    parts, weights = [], []
    for r in range(slots):
        column = [one[r] for one in lists]
        parts += [jnp.concatenate(column)] if width < WIDE else column
        weights += list(wide[r]) if isinstance(wide[r], tuple) else [wide[r]]
    here = core.reshape(1).astype(jnp.int32)
    theirs = swap(project(1 - here, parts, weights, jnp.bfloat16))
    mine = project(here, parts, weights, jnp.float32)
    return (mine + theirs.astype(jnp.float32)).astype(jnp.bfloat16)


def solution(mesh):
    count = mesh.shape["dp"]
    chips = mesh.shape["ctx"] // 2
    fine = Mesh(mesh.devices.reshape(count, chips, 2), ("dp", "z", "core"))
    every = ("dp", "z", "core")
    in_specs = (P(every, None), P(None, every, None), P(), P(), P(every, None))
    return jax.shard_map(
        functools.partial(shards, chips),
        mesh=fine,
        in_specs=in_specs,
        out_specs=P(every, None),
        check_vma=False,
    )
```

time: 206 us -> 195 us (0.947)
  starting transfers between devices: 76.9 us -> 62.8 us
  between operations: 3.03 us -> 13.7 us
  local copies, waits for them, and re-layouts: 18.8 us -> 9.9 us
  waiting for transfers between devices: 53.8 us -> 59.6 us
  Pallas kernels: 51 us -> 46.8 us
    ppermute x6, waiting for transfers between devices: 11.8 us -> 34.2 us  [shards(): forward = lambda block: lax.ppermute(block, 'z', ring)]
    ppermute x31 -> x19, waiting for transfers between devices: 42 us -> 24.7 us  [across(): return lax.ppermute(block, 'dp', [(i, i ^ r) for i in range(count)])]
    ppermute x31 -> x19, starting transfers between devices: 39.8 us -> 23 us  [across(): return lax.ppermute(block, 'dp', [(i, i ^ r) for i in range(count)])]
    ppermute x7 -> x3, starting transfers between devices: 8.88 us -> 17 us  [swap(): return lax.ppermute(block, 'core', [(0, 1), (1, 0)])]
    unnamed x60 -> x23, local copies, waits for them, and re-layouts: 10.5 us -> 4.1 us
    ppermute x6, starting transfers between devices: 26.9 us -> 21.4 us  [shards(): forward = lambda block: lax.ppermute(block, 'z', ring)]
    pallas_call x6, Pallas kernels: 51 us -> 46.8 us  [the longest x4 38 us: mix_chunk(): pl.pallas_call(functools.partial(mix_kernel, step, slots), out_shape=[jax...]
    pad x4 -> x0, local copies, waits for them, and re-layouts: 3.73 us -> none  [shards(): taps.append(jnp.pad(part.reshape(SHORT, 3 * width).T, ((0, 0), (0, 1))))]
  transfers between devices with their start and end apart: 46 -> 31, of which waited for: 11 -> 9; matrix products, arithmetic and copies ran while one was open for 4% -> 3% of each run, Pallas kernels for 23% -> 22%
where the time goes in v1:
time: 195 us
  starting transfers between devices  62.8 us (32%)
  waiting for transfers between devices  59.6 us (31%)
  Pallas kernels  46.8 us (24%)
  between operations  13.7 us (7%)
  local copies, waits for them, and re-layouts  9.9 us (5%)
    pallas_call x4, Pallas kernels, mix_chunk(): pl.pallas_call(functools.partial(mix_kernel, step, slots), out_shape=[jax...  38 us
    ppermute x6, waiting for transfers between devices, shards(): forward = lambda block: lax.ppermute(block, 'z', ring)  34.2 us
    ppermute x19, waiting for transfers between devices, across(): return lax.ppermute(block, 'dp', [(i, i ^ r) for i in range(count)])  24.7 us
    ppermute x19, starting transfers between devices, across(): return lax.ppermute(block, 'dp', [(i, i ^ r) for i in range(count)])  23 us
    ppermute x6, starting transfers between devices, shards(): forward = lambda block: lax.ppermute(block, 'z', ring)  21.4 us
    ppermute x3, starting transfers between devices, swap(): return lax.ppermute(block, 'core', [(0, 1), (1, 0)])  17 us
    pallas_call x2, Pallas kernels, project(): pl.pallas_call(functools.partial(out_kernel, counts), out_shape=jax.Shape...  8.78 us
    unnamed x23, local copies, waits for them, and re-layouts  4.1 us
  transfers between devices with their start and end apart: 31, of which 9 were waited for; matrix products, arithmetic and copies ran while one was open for 3% of the time, Pallas kernels for 22%

profile of v1, /device:TPU:0, one launch (start us, length us, event | category | flops | bytes accessed | tf_op | source)
XLA Modules:
  0.0 194.6 jit_solution(15861422344578251333)
XLA Ops:
  6.5 0.7 all-gather.3.cloned.1.call-update
  7.3 1.1 fusion.5
  8.4 0.7 collective-permute-start
  9.1 0.7 collective-permute-start.1
  9.9 4.0 %collective-permute-start.4 = (bf16[144,1024]{1,0:T(8,128)(2,1)S(1)}, bf16[144,1024]{1,0:T(8,128)(2,1)S(1)}, u32[]{:S(2)}, u32[]{:S(2)}) collective-permute-start(bf16[144,1024]{1,0:T(8,128)(2,1)S(1)} %add.69), channel_id=1, source_target_pairs={{0,24},{8,16},{16,8},{24,0},{1,25},{9,17},{17,9},{25,1},{2,26},{10... | collective-permute-start | bytes 884744 | tf_op jit(solution)/shard_map/ppermute | solution.py:42
  14.5 8.6 %collective-permute-start.9 = (bf16[3,64,2048]{2,1,0:T(8,128)(2,1)S(1)}, bf16[3,64,2048]{2,1,0:T(8,128)(2,1)S(1)}, u32[]{:S(2)}, u32[]{:S(2)}) collective-permute-start(bf16[3,64,2048]{2,1,0:T(8,128)(2,1)S(1)} %copy-done.3), channel_id=1, source_target_pairs={{0,2},{2,6},{6,4},{4,0},{1,3},{3,7},{7,5},{5,1},{8,10},{10,14},{14... | collective-permute-start | bytes 2359304 | tf_op jit(solution)/shard_map/ppermute | solution.py:247
  23.5 16.9 %collective-permute-start.5 = (bf16[4,144,1024]{2,1,0:T(8,128)(2,1)S(1)}, bf16[4,144,1024]{2,1,0:T(8,128)(2,1)S(1)}, u32[]{:S(2)}, u32[]{:S(2)}) collective-permute-start(bf16[4,144,1024]{2,1,0:T(8,128)(2,1)S(1)} %pad_maximum_fusion.rest_2_), channel_id=1, source_target_pairs={{0,1},{1,0},{2,3},{3,2},{4,5},{5,4},{6,7},{7,6},{8,9},{9,8},{10,11... | collective-permute-start | bytes 3538952 | tf_op jit(solution)/shard_map/ppermute | solution.py:37
  40.4 7.8 %collective-permute-start.6 = (bf16[64,2048]{1,0:T(8,128)(2,1)S(1)}, bf16[64,2048]{1,0:T(8,128)(2,1)S(1)}, u32[]{:S(2)}, u32[]{:S(2)}) collective-permute-start(bf16[64,2048]{1,0:T(8,128)(2,1)S(1)} %copy-done.9), channel_id=1, source_target_pairs={{0,2},{2,6},{6,4},{4,0},{1,3},{3,7},{7,5},{5,1},{8,10},{10,14},{14... | collective-permute-start | bytes 786440 | tf_op jit(solution)/shard_map/ppermute | solution.py:247
  48.2 2.4 %collective-permute-start.10 = (bf16[3,64,2048]{2,1,0:T(8,128)(2,1)S(1)}, bf16[3,64,2048]{2,1,0:T(8,128)(2,1)S(1)}, u32[]{:S(2)}, u32[]{:S(2)}) collective-permute-start(bf16[3,64,2048]{2,1,0:T(8,128)(2,1)S(1)} %collective-permute-done.9), channel_id=1, source_target_pairs={{0,2},{2,6},{6,4},{4,0},{1,3},{3,7},{7,5},{5,1},{8,10},{10,14},{14... | collective-permute-start | bytes 2359304 | tf_op jit(solution)/shard_map/ppermute | solution.py:247
  50.6 5.6 %collective-permute-done.6 = bf16[64,2048]{1,0:T(8,128)(2,1)S(1)} collective-permute-done((bf16[64,2048]{1,0:T(8,128)(2,1)S(1)}, bf16[64,2048]{1,0:T(8,128)(2,1)S(1)}, u32[]{:S(2)}, u32[]{:S(2)}) %collective-permute-start.6) | collective-permute-done | bytes 262176 | tf_op jit(solution)/shard_map/ppermute | solution.py:247
  56.2 1.2 collective-permute-start.7
  57.4 20.8 %collective-permute-done.7 = bf16[64,2048]{1,0:T(8,128)(2,1)S(1)} collective-permute-done((bf16[64,2048]{1,0:T(8,128)(2,1)S(1)}, bf16[64,2048]{1,0:T(8,128)(2,1)S(1)}, u32[]{:S(2)}, u32[]{:S(2)}) %collective-permute-start.7) | collective-permute-done | bytes 262176 | tf_op jit(solution)/shard_map/ppermute | solution.py:247
  78.2 0.8 collective-permute-start.8
  79.0 7.8 %collective-permute-done.8 = bf16[64,2048]{1,0:T(8,128)(2,1)S(1)} collective-permute-done((bf16[64,2048]{1,0:T(8,128)(2,1)S(1)}, bf16[64,2048]{1,0:T(8,128)(2,1)S(1)}, u32[]{:S(2)}, u32[]{:S(2)}) %collective-permute-start.8) | collective-permute-done | bytes 262176 | tf_op jit(solution)/shard_map/ppermute | solution.py:247
  86.9 0.9 copy-done.7
  87.8 1.0 copy-done.1
  88.8 1.0 reshape.23
  90.4 1.5 collective-permute-start.26
  91.9 0.9 constant_dynamic-slice_fusion.4
  92.9 0.8 fusion.4
  93.8 0.8 fusion
  95.3 20.4 %collective-permute-done.26.refs_18_ = bf16[256,2048]{1,0:T(8,128)(2,1)} collective-permute-done((bf16[256,2048]{1,0:T(8,128)(2,1)S(1)}, bf16[256,2048]{1,0:T(8,128)(2,1)}, u32[]{:S(2)}, u32[]{:S(2)}) %collective-permute-start.26) | collective-permute-done | bytes 1048608 | tf_op jit(solution)/shard_map/ppermute | solution.py:42
  115.8 1.1 slice.34
  116.9 1.5 collective-permute-start.27
  118.4 0.9 collective-permute-start.28
  119.4 2.2 %copy-done = bf16[1024,2048]{1,0:T(8,128)(2,1)S(1)} copy-done((bf16[1024,2048]{1,0:T(8,128)(2,1)S(1)}, bf16[1024,2048]{1,0:T(8,128)(2,1)}, u32[]{:S(2)}) %copy-start) | copy-done | bytes 4194328
  121.5 9.5 %shard_map.64 = (bf16[64,512]{1,0:T(8,128)(2,1)S(1)}, bf16[64,512]{1,0:T(8,128)(2,1)S(1)}, bf16[64,512]{1,0:T(8,128)(2,1)S(1)}, bf16[64,512]{1,0:T(8,128)(2,1)S(1)}) custom-call(s32[6]{0:T(128)S(1)} %pad_add_fusion.place_ref, bf16[192,2048]{1,0:T(8,128)(2,1)S(1)} %bitcast.39, f32[4,8,256]{2,1,0:T(8,128)S(1)} %pad_maximum_fusion.2.taps_ref, ...), custom_call_target="tpu_custom_call" | custom-call | flops 4294967296 | bytes 8388608 | tf_op jit(solution)/shard_map/pallas_call | solution.py:162
  131.1 1.3 collective-permute-start.13
  132.3 9.5 %shard_map.65 = (bf16[64,512]{1,0:T(8,128)(2,1)S(1)}, bf16[64,512]{1,0:T(8,128)(2,1)S(1)}, bf16[64,512]{1,0:T(8,128)(2,1)S(1)}, bf16[64,512]{1,0:T(8,128)(2,1)S(1)}) custom-call(s32[6]{0:T(128)S(1)} %pad_add_fusion.place_ref, bf16[192,2048]{1,0:T(8,128)(2,1)S(1)} %bitcast.40, f32[4,8,256]{2,1,0:T(8,128)S(1)} %pad_maximum_fusion.2.taps_ref, ...), custom_call_target="tpu_custom_call" | custom-call | flops 4294967296 | bytes 8388608 | tf_op jit(solution)/shard_map/pallas_call | solution.py:162
  141.8 0.9 collective-permute-start.14
  142.7 9.5 %shard_map.66 = (bf16[64,512]{1,0:T(8,128)(2,1)S(1)}, bf16[64,512]{1,0:T(8,128)(2,1)S(1)}, bf16[64,512]{1,0:T(8,128)(2,1)S(1)}, bf16[64,512]{1,0:T(8,128)(2,1)S(1)}) custom-call(s32[6]{0:T(128)S(1)} %pad_add_fusion.place_ref, bf16[192,2048]{1,0:T(8,128)(2,1)S(1)} %bitcast.41, f32[4,8,256]{2,1,0:T(8,128)S(1)} %pad_maximum_fusion.2.taps_ref, ...), custom_call_target="tpu_custom_call" | custom-call | flops 4294967296 | bytes 8388608 | tf_op jit(solution)/shard_map/pallas_call | solution.py:162
  152.2 1.3 collective-permute-start.15
  153.5 9.5 %shard_map.67 = (bf16[64,512]{1,0:T(8,128)(2,1)S(1)}, bf16[64,512]{1,0:T(8,128)(2,1)S(1)}, bf16[64,512]{1,0:T(8,128)(2,1)S(1)}, bf16[64,512]{1,0:T(8,128)(2,1)S(1)}) custom-call(s32[6]{0:T(128)S(1)} %pad_add_fusion.place_ref, bf16[192,2048]{1,0:T(8,128)(2,1)S(1)} %bitcast.42, f32[4,8,256]{2,1,0:T(8,128)S(1)} %pad_maximum_fusion.2.taps_ref, ...), custom_call_target="tpu_custom_call" | custom-call | flops 4294967296 | bytes 8388608 | tf_op jit(solution)/shard_map/pallas_call | solution.py:162
  163.0 0.9 collective-permute-start.16
  163.9 1.2 collective-permute-start.17
  165.1 0.8 collective-permute-start.18
  166.0 1.2 collective-permute-start.19
  167.2 0.8 collective-permute-start.20
  168.0 1.2 collective-permute-start.21
  169.2 1.7 collective-permute-start.22
  170.9 1.2 collective-permute-start.23
  172.4 1.5 collective-permute-start.24
  173.9 0.7 collective-permute-done.20.refs_11_
  174.5 1.6 collective-permute-done.23.refs_14_
  176.1 1.5 collective-permute-done.24.refs_15_
  177.6 4.4 %shard_map.69 = bf16[256,2048]{1,0:T(8,128)(2,1)S(1)} custom-call(s32[1]{0:T(128)S(6)} %sub.20.core_ref, bf16[64,512]{1,0:T(8,128)(2,1)S(1)} %get-tuple-element.27.refs_0_, bf16[64,512]{1,0:T(8,128)(2,1)S(1)} %get-tuple-element.28.refs_1_, bf16[64,512]{1,0:T(8,128)(2,1)S(1)} %get-tuple-element.30.refs_2_, bf16[64,512]{1,0:T(8,128)(2,1)S(1)} %get-tuple-element.31.refs_3_, ...), custom_call_target="tpu_custom_call" | custom-call | flops 2147483648 | bytes 5242880 | tf_op jit(solution)/shard_map/pallas_call | solution.py:215
  182.0 4.4 %shard_map.68 = f32[256,2048]{1,0:T(8,128)S(1)} custom-call(s32[1]{0:T(128)} %bitcast.core_ref, bf16[64,512]{1,0:T(8,128)(2,1)S(1)} %get-tuple-element.27.refs_0_, bf16[64,512]{1,0:T(8,128)(2,1)S(1)} %get-tuple-element.28.refs_1_, bf16[64,512]{1,0:T(8,128)(2,1)S(1)} %get-tuple-element.30.refs_2_, bf16[64,512]{1,0:T(8,128)(2,1)S(1)} %get-tuple-element.31.refs_3_, ...), custom_call_target="tpu_custom_call" | custom-call | flops 2147483648 | bytes 5242880 | tf_op jit(solution)/shard_map/pallas_call | solution.py:215
  186.5 1.3 add_convert_fusion
  (62 shorter events, 3.0 us)
Async XLA Ops:
  6.5 8.0 %copy-start.3 = (bf16[3,64,2048]{2,1,0:T(8,128)(2,1)S(1)}, bf16[3,64,2048]{2,1,0:T(8,128)(2,1)}, u32[]{:S(2)}) copy-start(bf16[3,64,2048]{2,1,0:T(8,128)(2,1)} %param.7) | copy-start | bytes 2359300
  6.5 82.3 %all-gather.3.cloned.1.call-start = ((), (), s32[]{:S(2)}) async-start(), calls=%async_computation | async-start | bytes 5242880 | tf_op jit(solution)/shard_map/all_gather | solution.py:273
  7.3 33.1 %copy-start.9 = (bf16[64,2048]{1,0:T(8,128)(2,1)S(1)}, bf16[64,2048]{1,0:T(8,128)(2,1)}, u32[]{:S(2)}) copy-start(bf16[64,2048]{1,0:T(8,128)(2,1)} %param.10) | copy-start | bytes 786436
  8.4 1.4 collective-permute-start
  9.1 0.7 collective-permute-start.1
  9.9 13.2 %collective-permute-start.4 = (bf16[144,1024]{1,0:T(8,128)(2,1)S(1)}, bf16[144,1024]{1,0:T(8,128)(2,1)S(1)}, u32[]{:S(2)}, u32[]{:S(2)}) collective-permute-start(bf16[144,1024]{1,0:T(8,128)(2,1)S(1)} %add.69), channel_id=1, source_target_pairs={{0,24},{8,16},{16,8},{24,0},{1,25},{9,17},{17,9},{25,1},{2,26},{10... | collective-permute-start | bytes 884744 | tf_op jit(solution)/shard_map/ppermute | solution.py:42
  13.8 9.3 %collective-permute-start.3 = (bf16[144,1024]{1,0:T(8,128)(2,1)S(1)}, bf16[144,1024]{1,0:T(8,128)(2,1)S(1)}, u32[]{:S(2)}, u32[]{:S(2)}) collective-permute-start(bf16[144,1024]{1,0:T(8,128)(2,1)S(1)} %add.69), channel_id=1, source_target_pairs={{0,16},{8,24},{16,0},{24,8},{1,17},{9,25},{17,1},{25,9},{2,18},{10... | collective-permute-start | bytes 884744 | tf_op jit(solution)/shard_map/ppermute | solution.py:42
  14.4 9.0 %collective-permute-start.2 = (bf16[144,1024]{1,0:T(8,128)(2,1)S(1)}, bf16[144,1024]{1,0:T(8,128)(2,1)S(1)}, u32[]{:S(2)}, u32[]{:S(2)}) collective-permute-start(bf16[144,1024]{1,0:T(8,128)(2,1)S(1)} %add.69), channel_id=1, source_target_pairs={{0,8},{8,0},{16,24},{24,16},{1,9},{9,1},{17,25},{25,17},{2,10},{10... | collective-permute-start | bytes 884744 | tf_op jit(solution)/shard_map/ppermute | solution.py:42
  14.5 33.7 %collective-permute-start.9 = (bf16[3,64,2048]{2,1,0:T(8,128)(2,1)S(1)}, bf16[3,64,2048]{2,1,0:T(8,128)(2,1)S(1)}, u32[]{:S(2)}, u32[]{:S(2)}) collective-permute-start(bf16[3,64,2048]{2,1,0:T(8,128)(2,1)S(1)} %copy-done.3), channel_id=1, source_target_pairs={{0,2},{2,6},{6,4},{4,0},{1,3},{3,7},{7,5},{5,1},{8,10},{10,14},{14... | collective-permute-start | bytes 2359304 | tf_op jit(solution)/shard_map/ppermute | solution.py:247
  23.3 65.5 %copy-start.10 = (f32[7,3,2048]{2,0,1:T(8,128)S(1)}, f32[7,3,2048]{2,0,1:T(8,128)}, u32[]{:S(2)}) copy-start(f32[7,3,2048]{2,0,1:T(8,128)} %param.8) | copy-start | bytes 516100
  23.5 64.3 %collective-permute-start.5 = (bf16[4,144,1024]{2,1,0:T(8,128)(2,1)S(1)}, bf16[4,144,1024]{2,1,0:T(8,128)(2,1)S(1)}, u32[]{:S(2)}, u32[]{:S(2)}) collective-permute-start(bf16[4,144,1024]{2,1,0:T(8,128)(2,1)S(1)} %pad_maximum_fusion.rest_2_), channel_id=1, source_target_pairs={{0,1},{1,0},{2,3},{3,2},{4,5},{5,4},{6,7},{7,6},{8,9},{9,8},{10,11... | collective-permute-start | bytes 3538952 | tf_op jit(solution)/shard_map/ppermute | solution.py:37
  40.4 15.8 %collective-permute-start.6 = (bf16[64,2048]{1,0:T(8,128)(2,1)S(1)}, bf16[64,2048]{1,0:T(8,128)(2,1)S(1)}, u32[]{:S(2)}, u32[]{:S(2)}) collective-permute-start(bf16[64,2048]{1,0:T(8,128)(2,1)S(1)} %copy-done.9), channel_id=1, source_target_pairs={{0,2},{2,6},{6,4},{4,0},{1,3},{3,7},{7,5},{5,1},{8,10},{10,14},{14... | collective-permute-start | bytes 786440 | tf_op jit(solution)/shard_map/ppermute | solution.py:247
  48.2 41.6 %copy-start.5 = (bf16[3,64,2048]{2,1,0:T(8,128)(2,1)}, bf16[3,64,2048]{2,1,0:T(8,128)(2,1)S(1)}, u32[]{:S(2)}) copy-start(bf16[3,64,2048]{2,1,0:T(8,128)(2,1)S(1)} %collective-permute-done.9) | copy-start | bytes 2359300
  48.2 38.7 %collective-permute-start.10 = (bf16[3,64,2048]{2,1,0:T(8,128)(2,1)S(1)}, bf16[3,64,2048]{2,1,0:T(8,128)(2,1)S(1)}, u32[]{:S(2)}, u32[]{:S(2)}) collective-permute-start(bf16[3,64,2048]{2,1,0:T(8,128)(2,1)S(1)} %collective-permute-done.9), channel_id=1, source_target_pairs={{0,2},{2,6},{6,4},{4,0},{1,3},{3,7},{7,5},{5,1},{8,10},{10,14},{14... | collective-permute-start | bytes 2359304 | tf_op jit(solution)/shard_map/ppermute | solution.py:247
  56.2 21.9 %collective-permute-start.7 = (bf16[64,2048]{1,0:T(8,128)(2,1)S(1)}, bf16[64,2048]{1,0:T(8,128)(2,1)S(1)}, u32[]{:S(2)}, u32[]{:S(2)}) collective-permute-start(bf16[64,2048]{1,0:T(8,128)(2,1)S(1)} %collective-permute-done.6), channel_id=1, source_target_pairs={{0,2},{2,6},{6,4},{4,0},{1,3},{3,7},{7,5},{5,1},{8,10},{10,14},{14... | collective-permute-start | bytes 786440 | tf_op jit(solution)/shard_map/ppermute | solution.py:247
  78.2 8.7 %collective-permute-start.8 = (bf16[64,2048]{1,0:T(8,128)(2,1)S(1)}, bf16[64,2048]{1,0:T(8,128)(2,1)S(1)}, u32[]{:S(2)}, u32[]{:S(2)}) collective-permute-start(bf16[64,2048]{1,0:T(8,128)(2,1)S(1)} %collective-permute-done.7), channel_id=1, source_target_pairs={{0,2},{2,6},{6,4},{4,0},{1,3},{3,7},{7,5},{5,1},{8,10},{10,14},{14... | collective-permute-start | bytes 786440 | tf_op jit(solution)/shard_map/ppermute | solution.py:247
  86.9 0.9 copy-start.7
  87.8 1.0 copy-start.1
  88.8 30.5 %collective-permute-start.11 = (bf16[4,256,2048]{2,1,0:T(8,128)(2,1)}, bf16[4,256,2048]{2,1,0:T(8,128)(2,1)}, u32[]{:S(2)}, u32[]{:S(2)}) collective-permute-start(bf16[4,256,2048]{2,1,0:T(8,128)(2,1)} %bitcast.34), channel_id=1, source_target_pairs={{0,1},{1,0},{2,3},{3,2},{4,5},{5,4},{6,7},{7,6},{8,9},{9,8},{10,11... | collective-permute-start | bytes 12582920 | tf_op jit(solution)/shard_map/ppermute | solution.py:37
  89.8 28.6 %collective-permute-start.25 = (bf16[256,2048]{1,0:T(8,128)(2,1)S(1)}, bf16[256,2048]{1,0:T(8,128)(2,1)S(1)}, u32[]{:S(2)}, u32[]{:S(2)}) collective-permute-start(bf16[256,2048]{1,0:T(8,128)(2,1)S(1)} %pad_maximum_fusion.1.refs_16_), channel_id=1, source_target_pairs={{0,8},{8,0},{16,24},{24,16},{1,9},{9,1},{17,25},{25,17},{2,10},{10... | collective-permute-start | bytes 3145736 | tf_op jit(solution)/shard_map/ppermute | solution.py:42
  90.4 25.4 %collective-permute-start.26 = (bf16[256,2048]{1,0:T(8,128)(2,1)S(1)}, bf16[256,2048]{1,0:T(8,128)(2,1)}, u32[]{:S(2)}, u32[]{:S(2)}) collective-permute-start(bf16[256,2048]{1,0:T(8,128)(2,1)S(1)} %pad_maximum_fusion.1.refs_16_), channel_id=1, source_target_pairs={{0,16},{8,24},{16,0},{24,8},{1,17},{9,25},{17,1},{25,9},{2,18},{10... | collective-permute-start | bytes 3145736 | tf_op jit(solution)/shard_map/ppermute | solution.py:42
  92.9 26.5 %copy-start.2 = (bf16[4,144,1024]{2,1,0:T(8,128)(2,1)S(1)}, bf16[4,144,1024]{2,1,0:T(8,128)(2,1)}, u32[]{:S(2)}) copy-start(bf16[4,144,1024]{2,1,0:T(8,128)(2,1)} %copy-done.1) | copy-start | bytes 3538948
  92.9 26.4 %copy-start.4 = (bf16[3,64,2048]{2,1,0:T(8,128)(2,1)S(1)}, bf16[3,64,2048]{2,1,0:T(8,128)(2,1)}, u32[]{:S(2)}) copy-start(bf16[3,64,2048]{2,1,0:T(8,128)(2,1)} %param.7) | copy-start | bytes 2359300
  94.7 57.5 %collective-permute-start.12 = (bf16[3,64,2048]{2,1,0:T(8,128)(2,1)}, bf16[3,64,2048]{2,1,0:T(8,128)(2,1)S(1)}, u32[]{:S(2)}, u32[]{:S(2)}) collective-permute-start(bf16[3,64,2048]{2,1,0:T(8,128)(2,1)} %copy-done.7), channel_id=1, source_target_pairs={{0,2},{2,6},{6,4},{4,0},{1,3},{3,7},{7,5},{5,1},{8,10},{10,14},{14... | collective-permute-start | bytes 2359304 | tf_op jit(solution)/shard_map/ppermute | solution.py:247
  116.9 46.2 %collective-permute-start.27 = (bf16[128,2048]{1,0:T(8,128)(2,1)S(1)}, bf16[128,2048]{1,0:T(8,128)(2,1)S(1)}, u32[]{:S(2)}, u32[]{:S(2)}) collective-permute-start(bf16[128,2048]{1,0:T(8,128)(2,1)S(1)} %slice.34), channel_id=1, source_target_pairs={{0,8},{8,0},{16,24},{24,16},{1,9},{9,1},{17,25},{25,17},{2,10},{10... | collective-permute-start | bytes 1572872 | tf_op jit(solution)/shard_map/ppermute | solution.py:42
  118.4 45.5 %collective-permute-start.28 = (bf16[128,2048]{1,0:T(8,128)(2,1)S(1)}, bf16[128,2048]{1,0:T(8,128)(2,1)S(1)}, u32[]{:S(2)}, u32[]{:S(2)}) collective-permute-start(bf16[128,2048]{1,0:T(8,128)(2,1)S(1)} %slice.35), channel_id=1, source_target_pairs={{0,16},{8,24},{16,0},{24,8},{1,17},{9,25},{17,1},{25,9},{2,18},{10... | collective-permute-start | bytes 1572872 | tf_op jit(solution)/shard_map/ppermute | solution.py:42
  119.4 2.2 %copy-start = (bf16[1024,2048]{1,0:T(8,128)(2,1)S(1)}, bf16[1024,2048]{1,0:T(8,128)(2,1)}, u32[]{:S(2)}) copy-start(bf16[1024,2048]{1,0:T(8,128)(2,1)} %all-gather.3.cloned.1.call-done) | copy-start | bytes 12582916
  121.5 10.8 %copy-start.6 = (bf16[3,64,2048]{2,1,0:T(8,128)(2,1)S(1)}, bf16[3,64,2048]{2,1,0:T(8,128)(2,1)}, u32[]{:S(2)}) copy-start(bf16[3,64,2048]{2,1,0:T(8,128)(2,1)} %copy-done.5) | copy-start | bytes 2359300
  131.1 34.1 %collective-permute-start.13 = (bf16[64,512]{1,0:T(8,128)(2,1)S(1)}, bf16[64,512]{1,0:T(8,128)(2,1)S(1)}, u32[]{:S(2)}, u32[]{:S(2)}) collective-permute-start(bf16[64,512]{1,0:T(8,128)(2,1)S(1)} %get-tuple-element.32), channel_id=1, source_target_pairs={{0,8},{8,0},{16,24},{24,16},{1,9},{9,1},{17,25},{25,17},{2,10},{10... | collective-permute-start | bytes 196616 | tf_op jit(solution)/shard_map/ppermute | solution.py:42
  132.3 10.4 %copy-start.8 = (bf16[3,64,2048]{2,1,0:T(8,128)(2,1)S(1)}, bf16[3,64,2048]{2,1,0:T(8,128)(2,1)}, u32[]{:S(2)}) copy-start(bf16[3,64,2048]{2,1,0:T(8,128)(2,1)} %copy-done.7) | copy-start | bytes 2359300
  141.8 24.1 %collective-permute-start.14 = (bf16[64,512]{1,0:T(8,128)(2,1)S(1)}, bf16[64,512]{1,0:T(8,128)(2,1)S(1)}, u32[]{:S(2)}, u32[]{:S(2)}) collective-permute-start(bf16[64,512]{1,0:T(8,128)(2,1)S(1)} %get-tuple-element.33), channel_id=1, source_target_pairs={{0,8},{8,0},{16,24},{24,16},{1,9},{9,1},{17,25},{25,17},{2,10},{10... | collective-permute-start | bytes 196616 | tf_op jit(solution)/shard_map/ppermute | solution.py:42
  152.2 14.9 %collective-permute-start.15 = (bf16[64,512]{1,0:T(8,128)(2,1)S(1)}, bf16[64,512]{1,0:T(8,128)(2,1)S(1)}, u32[]{:S(2)}, u32[]{:S(2)}) collective-permute-start(bf16[64,512]{1,0:T(8,128)(2,1)S(1)} %get-tuple-element.34), channel_id=1, source_target_pairs={{0,8},{8,0},{16,24},{24,16},{1,9},{9,1},{17,25},{25,17},{2,10},{10... | collective-permute-start | bytes 196616 | tf_op jit(solution)/shard_map/ppermute | solution.py:42
  163.0 5.0 %collective-permute-start.16 = (bf16[64,512]{1,0:T(8,128)(2,1)S(1)}, bf16[64,512]{1,0:T(8,128)(2,1)S(1)}, u32[]{:S(2)}, u32[]{:S(2)}) collective-permute-start(bf16[64,512]{1,0:T(8,128)(2,1)S(1)} %get-tuple-element.35), channel_id=1, source_target_pairs={{0,8},{8,0},{16,24},{24,16},{1,9},{9,1},{17,25},{25,17},{2,10},{10... | collective-permute-start | bytes 196616 | tf_op jit(solution)/shard_map/ppermute | solution.py:42
  163.9 5.2 %collective-permute-start.17 = (bf16[64,512]{1,0:T(8,128)(2,1)S(1)}, bf16[64,512]{1,0:T(8,128)(2,1)S(1)}, u32[]{:S(2)}, u32[]{:S(2)}) collective-permute-start(bf16[64,512]{1,0:T(8,128)(2,1)S(1)} %get-tuple-element.36), channel_id=1, source_target_pairs={{0,16},{8,24},{16,0},{24,8},{1,17},{9,25},{17,1},{25,9},{2,18},{10... | collective-permute-start | bytes 196616 | tf_op jit(solution)/shard_map/ppermute | solution.py:42
  165.1 5.8 %collective-permute-start.18 = (bf16[64,512]{1,0:T(8,128)(2,1)S(1)}, bf16[64,512]{1,0:T(8,128)(2,1)S(1)}, u32[]{:S(2)}, u32[]{:S(2)}) collective-permute-start(bf16[64,512]{1,0:T(8,128)(2,1)S(1)} %get-tuple-element.37), channel_id=1, source_target_pairs={{0,16},{8,24},{16,0},{24,8},{1,17},{9,25},{17,1},{25,9},{2,18},{10... | collective-permute-start | bytes 196616 | tf_op jit(solution)/shard_map/ppermute | solution.py:42
  166.0 6.4 %collective-permute-start.19 = (bf16[64,512]{1,0:T(8,128)(2,1)S(1)}, bf16[64,512]{1,0:T(8,128)(2,1)S(1)}, u32[]{:S(2)}, u32[]{:S(2)}) collective-permute-start(bf16[64,512]{1,0:T(8,128)(2,1)S(1)} %get-tuple-element.38), channel_id=1, source_target_pairs={{0,16},{8,24},{16,0},{24,8},{1,17},{9,25},{17,1},{25,9},{2,18},{10... | collective-permute-start | bytes 196616 | tf_op jit(solution)/shard_map/ppermute | solution.py:42
  167.2 7.4 %collective-permute-start.20 = (bf16[64,512]{1,0:T(8,128)(2,1)S(1)}, bf16[64,512]{1,0:T(8,128)(2,1)S(1)}, u32[]{:S(2)}, u32[]{:S(2)}) collective-permute-start(bf16[64,512]{1,0:T(8,128)(2,1)S(1)} %get-tuple-element.39), channel_id=1, source_target_pairs={{0,16},{8,24},{16,0},{24,8},{1,17},{9,25},{17,1},{25,9},{2,18},{10... | collective-permute-start | bytes 196616 | tf_op jit(solution)/shard_map/ppermute | solution.py:42
  168.0 6.5 %collective-permute-start.21 = (bf16[64,512]{1,0:T(8,128)(2,1)S(1)}, bf16[64,512]{1,0:T(8,128)(2,1)S(1)}, u32[]{:S(2)}, u32[]{:S(2)}) collective-permute-start(bf16[64,512]{1,0:T(8,128)(2,1)S(1)} %get-tuple-element.40), channel_id=1, source_target_pairs={{0,24},{8,16},{16,8},{24,0},{1,25},{9,17},{17,9},{25,1},{2,26},{10... | collective-permute-start | bytes 196616 | tf_op jit(solution)/shard_map/ppermute | solution.py:42
  169.2 5.3 %collective-permute-start.22 = (bf16[64,512]{1,0:T(8,128)(2,1)S(1)}, bf16[64,512]{1,0:T(8,128)(2,1)S(1)}, u32[]{:S(2)}, u32[]{:S(2)}) collective-permute-start(bf16[64,512]{1,0:T(8,128)(2,1)S(1)} %get-tuple-element.41), channel_id=1, source_target_pairs={{0,24},{8,16},{16,8},{24,0},{1,25},{9,17},{17,9},{25,1},{2,26},{10... | collective-permute-start | bytes 196616 | tf_op jit(solution)/shard_map/ppermute | solution.py:42
  170.9 5.2 %collective-permute-start.23 = (bf16[64,512]{1,0:T(8,128)(2,1)S(1)}, bf16[64,512]{1,0:T(8,128)(2,1)S(1)}, u32[]{:S(2)}, u32[]{:S(2)}) collective-permute-start(bf16[64,512]{1,0:T(8,128)(2,1)S(1)} %get-tuple-element.42), channel_id=1, source_target_pairs={{0,24},{8,16},{16,8},{24,0},{1,25},{9,17},{17,9},{25,1},{2,26},{10... | collective-permute-start | bytes 196616 | tf_op jit(solution)/shard_map/ppermute | solution.py:42
  172.4 5.2 %collective-permute-start.24 = (bf16[64,512]{1,0:T(8,128)(2,1)S(1)}, bf16[64,512]{1,0:T(8,128)(2,1)S(1)}, u32[]{:S(2)}, u32[]{:S(2)}) collective-permute-start(bf16[64,512]{1,0:T(8,128)(2,1)S(1)} %get-tuple-element.43), channel_id=1, source_target_pairs={{0,24},{8,16},{16,8},{24,0},{1,25},{9,17},{17,9},{25,1},{2,26},{10... | collective-permute-start | bytes 196616 | tf_op jit(solution)/shard_map/ppermute | solution.py:42
  182.0 4.5 %collective-permute-start.29 = (bf16[256,2048]{1,0:T(8,128)(2,1)S(1)}, bf16[256,2048]{1,0:T(8,128)(2,1)S(1)}, u32[]{:S(2)}, u32[]{:S(2)}) collective-permute-start(bf16[256,2048]{1,0:T(8,128)(2,1)S(1)} %shard_map.69), channel_id=1, source_target_pairs={{0,1},{1,0},{2,3},{3,2},{4,5},{5,4},{6,7},{7,6},{8,9},{9,8},{10,11... | collective-permute-start | bytes 3145736 | tf_op jit(solution)/shard_map/ppermute | solution.py:37
Sparse Core Ops, SparseCore 0:
  9.2 68.0 all-gather.2
